TPU v7x, 128 devices: a whole 4x4x4 slice. The times are simulated.
128 devices in a mesh: row: 8 (over y, z_hi), col: 16 (over z_lo, x, core).
Axes of the slice: x: 4, y: 4, z: 4 (z_hi: 2, z_lo: 2; z = z_hi * 2 + z_lo), core: 2. Of those that a mesh axis runs over, the one named last changes fastest.
Arguments:
- counts: int32 [256, 32768], P('col', 'row'), may hold values from 0 to 1591, as said below
- whiten: bfloat16 [64, 512, 512], P('row'), may hold values from -0.75 to 0.75
- initial_tiles: float32 [8, 16, 96, 128, 128], P('row', 'col'), as said below
- tile_rows: int32 [8, 16, 96], P('row', 'col'), may hold values from 0 to 31, as said below
- tile_cols: int32 [8, 16, 96], P('row', 'col'), may hold values from 0 to 15
- tile_count: int32 [8, 16], P('row', 'col'), may hold values from 16 to 96, as said below
Outputs:
- precision: float32 [8, 16, 96, 128, 128], P('row', 'col')
- last_grad: float32 [8, 16, 96, 128, 128], P('row', 'col')
Inputs may be any that keep to these rules, and one draw needn't show every extreme that they name: Nonnegative k-mer counts. `tile_rows`: with tile_cols, the slots of one device name distinct tiles of its 32 x 16 grid; every tile on the global diagonal is named by a live slot. `tile_count`: some device has 96 live slots. `initial_tiles`: diagonal entries of diagonal tiles lie between 0.5 and 2.
All inputs are finite; a program needn't handle non-finite values.
Results may differ from a plain program's by a relative error of at most 0.025.
Values may be sent and summed in bfloat16 or wider, within the bound.
A program may use at most 192 MiB of HBM per device.

v0:
```python
import jax
import jax.numpy as jnp
from jax import lax
from jax.sharding import PartitionSpec as P

ITERS = 2


step_size = 0.08
penalty = 1.0
epsilon = 1e-05


def broadcast(block, axis, holder):
    block = jnp.where(lax.axis_index(axis) == holder, block, jnp.zeros_like(block))
    return lax.psum(block, axis)


def local(counts, whiten, initial_tiles, tile_rows, tile_cols, tile_count):
    row_count = lax.axis_size("row")
    col_count = lax.axis_size("col")
    local_samples = counts.shape[0]
    samples = local_samples * col_count
    row_width = counts.shape[1]
    col_width = row_width * row_count // col_count
    tile_size = initial_tiles.shape[-1]
    rows_grid = row_width // tile_size
    cols_grid = col_width // tile_size
    block_size = whiten.shape[-1]
    logged = jnp.log1p(counts.astype(jnp.float32))
    sums = lax.psum(jnp.sum(logged, axis=0), "col")
    feature_mean = sums / samples
    centered = logged - feature_mean
    variance = lax.psum(jnp.sum(centered * centered, axis=0), "col") / samples
    standard = (centered * lax.rsqrt(variance + epsilon)).astype(jnp.bfloat16)
    blocks = standard.reshape(local_samples, row_width // block_size, block_size)
    whitened = jnp.einsum("nbw,bwv->nbv", blocks, whiten, preferred_element_type=jnp.float32)
    whitened = whitened.astype(jnp.bfloat16).reshape(local_samples, row_width)
    col_index = lax.axis_index("col")
    row_index = lax.axis_index("row")
    group_ratio = col_count // row_count
    source_row = col_index // group_ratio
    offset = col_index % group_ratio * col_width
    row_x = lax.all_gather(whitened, "col", axis=0, tiled=True)
    column_x = broadcast(lax.dynamic_slice_in_dim(row_x, offset, col_width, 1), "row", source_row)
    row_x = row_x.reshape(samples, rows_grid, tile_size)
    column_x = column_x.reshape(samples, cols_grid, tile_size)
    slot_rows = tile_rows.reshape(-1)
    slot_cols = tile_cols.reshape(-1)
    slot_total = slot_rows.shape[0]
    live_slots = (jnp.arange(slot_total, dtype=jnp.int32) < tile_count.reshape(())).astype(
        jnp.float32
    )
    live_tiles = live_slots[:, None, None]
    omega = initial_tiles.reshape(slot_total, tile_size, tile_size) * live_tiles
    row_hot = (slot_rows[None, :] == jnp.arange(rows_grid, dtype=jnp.int32)[:, None]).astype(
        jnp.float32
    )
    col_hot = (slot_cols[None, :] == jnp.arange(cols_grid, dtype=jnp.int32)[:, None]).astype(
        jnp.float32
    )
    tile_diag = row_index * rows_grid + slot_rows == col_index * cols_grid + slot_cols
    identity = jnp.arange(tile_size)[:, None] == jnp.arange(tile_size)[None, :]
    on_diag = tile_diag[:, None, None] & identity[None, :, :]
    row_pick = jnp.take(row_x, slot_rows, axis=1)
    col_pick = jnp.take(column_x, slot_cols, axis=1)
    gradient = jnp.zeros_like(omega)
    for iteration in range(ITERS):
        omega_low = omega.astype(jnp.bfloat16)
        row_slots = jnp.einsum(
            "kaq,nkq->kan", omega_low, col_pick, preferred_element_type=jnp.float32
        )
        row_part = jnp.einsum("tk,kan->tan", row_hot, row_slots, precision=lax.Precision.HIGHEST)
        col_slots = jnp.einsum(
            "nka,kaq->knq", row_pick, omega_low, preferred_element_type=jnp.float32
        )
        col_part = jnp.einsum("sk,knq->nsq", col_hot, col_slots, precision=lax.Precision.HIGHEST)
        row_terms = lax.psum(row_part.astype(jnp.bfloat16), "col")
        column_terms = lax.psum(col_part.astype(jnp.bfloat16), "row")
        row_sel = jnp.take(row_terms, slot_rows, axis=0)
        col_sel = jnp.take(column_terms, slot_cols, axis=1)
        left = jnp.einsum("kan,nkq->kaq", row_sel, col_pick, preferred_element_type=jnp.float32)
        right = jnp.einsum("nka,nkq->kaq", row_pick, col_sel, preferred_element_type=jnp.float32)
        gradient = 0.5 * (left + right) / samples * live_tiles
        moved = omega - step_size * gradient
        shrunk = jnp.sign(moved) * jnp.maximum(jnp.abs(moved) - step_size * penalty, 0.0)
        diagonal = 0.5 * (moved + jnp.sqrt(moved * moved + 4.0 * step_size))
        omega = jnp.where(on_diag, diagonal, shrunk) * live_tiles
    out_shape = (1, 1, slot_total, tile_size, tile_size)
    return (omega.reshape(out_shape), gradient.reshape(out_shape))


def solution(mesh):
    in_specs = (
        P("col", "row"),
        P("row", None, None),
        P("row", "col", None, None, None),
        P("row", "col", None),
        P("row", "col", None),
        P("row", "col"),
    )
    out_specs = (P("row", "col", None, None, None), P("row", "col", None, None, None))
    return jax.shard_map(local, mesh=mesh, in_specs=in_specs, out_specs=out_specs, check_vma=False)
```

profile of v0, /device:TPU:1, one launch (start us, length us, event | category | flops | bytes accessed | tf_op | source)
XLA Modules:
  0.0 766.8 jit_solution(961645252021213039)
XLA Ops:
  7.2 0.0 all-gather.2.cloned.1.call-start
  7.2 1.1 fusion.72
  8.3 53.4 %psum.49 = f32[4096]{0:T(1024)S(1)} all-reduce(f32[4096]{0:T(1024)S(1)} %fusion.72), channel_id=1, replica_groups=mesh['row'=8,'col'=16] {'col'}, use_global_device_ids=true, to_apply=%region_1.0 | all-reduce | flops 4096 | bytes 32768 | tf_op jit(solution)/shard_map/psum | solution.py:31
  61.7 1.1 multiply_reduce_fusion
  62.8 52.9 %psum.50 = f32[4096]{0:T(1024)S(1)} all-reduce(f32[4096]{0:T(1024)S(1)} %multiply_reduce_fusion), channel_id=1, replica_groups=mesh['row'=8,'col'=16] {'col'}, use_global_device_ids=true, to_apply=%region_3.0 | all-reduce | flops 4096 | bytes 32768 | tf_op jit(solution)/shard_map/psum | solution.py:34
  115.7 1.1 multiply_convert_fusion
  116.7 2.8 fusion.70
  119.6 0.7 copy.56
  120.2 0.0 all-gather.2.cloned.1.call-update
  120.3 0.0 all-reduce.12.cloned.1.call-start
  121.0 0.7 fusion.85
  121.7 0.7 add_compare_fusion
  122.3 35.8 %all-gather.2.cloned.1.call-done = bf16[256,4096]{1,0:T(8,128)(2,1)} async-done(((bf16[16,4096]{1,0:T(8,128)(2,1)}), bf16[256,4096]{1,0:T(8,128)(2,1)}) %all-gather.2.cloned.1.call-update) | async-done | bytes 2097168 | tf_op jit(solution)/shard_map/all_gather | solution.py:44
  158.1 4.1 copy.39
  162.2 3.2 copy.40
  165.4 2.4 dynamic-slice_select_fusion
  167.8 1.5 copy.35
  169.3 1.3 copy.36
  170.6 6.5 gather_fusion
  177.1 6.5 fusion.19
  183.6 12.4 %fusion.67 = bf16[256,16,128]{2,1,0:T(8,128)(2,1)} fusion(f32[96,256,128]{2,1,0:T(8,128)S(1)} %fusion.19, s32[96]{0:T(128)S(1)} %bitcast.88), kind=kOutput, calls=%fused_computation.61 | convolution fusion | flops 604505600 | bytes 13631872 | tf_op jit(solution)/shard_map/sk,knq->nsq/dot_general | solution.py:77
  196.0 0.0 all-reduce.6.cloned.1.call-start
  196.1 108.4 %all-reduce.12.cloned.1.call-done = (bf16[256,16,128]{2,1,0:T(8,128)(2,1)}, bf16[256,16,128]{2,0,1:T(8,128)(2,1)}) async-done(((bf16[256,16,128]{2,1,0:T(8,128)(2,1)}, bf16[256,16,128]{2,0,1:T(8,128)(2,1)}), (bf16[256,16,128]{2,1,0:T(8,128)(2,1)}, bf16[256,16,128]{2,0,1:T(8,128)(2,1)})) %all-reduce.12.cloned.1.call-update) | async-done | bytes 2097168 | tf_op jit(solution)/shard_map/psum | solution.py:79
  304.5 7.2 gather_fusion.1
  311.6 11.0 %fusion.27 = f32[96,128,256]{2,1,0:T(8,128)} fusion(f32[1,1,96,128,128]{4,3,2,1,0:T(8,128)} %param.12, f32[96]{0:T(128)S(1)} %get-tuple-element.9, bf16[96,256,128]{2,1,0:T(8,128)(2,1)} %gather_fusion.1, pred[96]{0:T(512)(128)(4,1)S(1)} %get-tuple-element.8), kind=kOutput, calls=%fused_computation.35 | convolution fusion | flops 811597824 | bytes 25166304 | tf_op jit(solution)/shard_map/kaq,nkq->kan/dot_general | solution.py:70
  322.7 16.8 %fusion.46 = bf16[32,128,256]{2,0,1:T(8,128)(2,1)} fusion(f32[96,128,256]{2,1,0:T(8,128)} %fusion.27, s32[96]{0:T(128)S(1)} %bitcast.90), kind=kOutput, calls=%fused_computation.54 | convolution fusion | flops 1209011200 | bytes 14680448 | tf_op jit(solution)/shard_map/tk,kan->tan/dot_general | solution.py:73
  339.5 0.3 all-reduce.10.cloned.1.call-start
  339.9 0.8 copy.42
  340.7 6.0 gather_fusion.3
  346.7 9.5 %fusion.13 = f32[96,128,128]{2,1,0:T(8,128)} fusion(bf16[96,256,128]{1,2,0:T(8,128)(2,1)} %gather_fusion.3, pred[96]{0:T(512)(128)(4,1)S(1)} %get-tuple-element.8, bf16[96,256,128]{2,1,0:T(8,128)(2,1)} %gather_fusion, pred[96]{0:T(512)(128)(4,1)S(1)} %get-tuple-element.7), kind=kOutput, calls=%fused_computation.21 | convolution fusion | flops 811597824 | bytes 18874560 | tf_op jit(solution)/shard_map/nka,nkq->kaq/dot_general | solution.py:83
  356.2 109.0 %all-reduce.6.cloned.1.call-done = bf16[32,128,256]{2,0,1:T(8,128)(2,1)} async-done(((bf16[32,128,256]{2,0,1:T(8,128)(2,1)}), bf16[32,128,256]{2,0,1:T(8,128)(2,1)}) %all-reduce.6.cloned.1.call-update) | async-done | bytes 2097168 | tf_op jit(solution)/shard_map/psum | solution.py:78
  465.2 4.1 copy.38
  469.3 7.8 %gather_fusion.2 = bf16[96,128,256]{2,1,0:T(8,128)(2,1)} fusion(bf16[32,128,256]{2,1,0:T(8,128)(2,1)} %copy.38, s32[1024]{0:T(1024)S(1)} %pad_clamp_fusion.1), kind=kCustom, calls=%fused_computation.1.clone | custom fusion | bytes 12583296 | tf_op jit(solution)/shard_map/jit(_take)/gather | solution.py:80
  477.1 13.1 %fusion.8 = f32[96,128,128]{2,1,0:T(8,128)S(1)} fusion(f32[96,128,128]{2,1,0:T(8,128)} %fusion.13, f32[1,1,96,128,128]{4,3,2,1,0:T(8,128)} %param.12, f32[96]{0:T(128)S(1)} %compare_select_fusion.3, f32[96]{0:T(128)S(1)} %get-tuple-element.9, pred[128,128]{1,0:T(8,128)(4,1)S(1)} %iota_compare_fusion, pred[96]{0:T(512)(128)(4,1)S(1)} %get-tuple-element.6, ...), kind=kOutput, calls=%fused_computation.16 | convolution fusion | flops 838336512 | bytes 31474720 | tf_op jit(solution)/shard_map/kan,nkq->kaq/dot_general | solution.py:82
  490.2 6.4 fusion.16
  496.7 16.1 %fusion.64 = bf16[256,16,128]{2,1,0:T(8,128)(2,1)} fusion(f32[96,256,128]{2,1,0:T(8,128)} %fusion.16, s32[96]{0:T(128)S(1)} %bitcast.89), kind=kOutput, calls=%fused_computation.60 | convolution fusion | flops 604505600 | bytes 13631872 | tf_op jit(solution)/shard_map/sk,knq->nsq/dot_general | solution.py:77
  512.7 0.0 all-reduce.8.cloned.1.call-start
  512.8 11.0 %fusion.23 = f32[96,128,256]{2,1,0:T(8,128)} fusion(f32[96,128,128]{2,1,0:T(8,128)} %copy-done, bf16[96,256,128]{2,1,0:T(8,128)(2,1)} %gather_fusion.1, pred[96]{0:T(512)(128)(4,1)S(1)} %get-tuple-element.8), kind=kOutput, calls=%fused_computation.31 | convolution fusion | flops 810024960 | bytes 25165920 | tf_op jit(solution)/shard_map/kaq,nkq->kan/dot_general | solution.py:70
  523.8 16.9 %fusion.49 = bf16[32,128,256]{2,0,1:T(8,128)(2,1)} fusion(f32[96,128,256]{2,1,0:T(8,128)} %fusion.23, s32[96]{0:T(128)S(1)} %bitcast.91), kind=kOutput, calls=%fused_computation.55 | convolution fusion | flops 1209011200 | bytes 14680448 | tf_op jit(solution)/shard_map/tk,kan->tan/dot_general | solution.py:73
  540.7 57.4 %all-reduce.10.cloned.1.call-done = bf16[256,16,128]{2,1,0:T(8,128)(2,1)} async-done(((bf16[256,16,128]{2,1,0:T(8,128)(2,1)}), bf16[256,16,128]{2,1,0:T(8,128)(2,1)}) %all-reduce.10.cloned.1.call-update) | async-done | bytes 1048592 | tf_op jit(solution)/shard_map/psum | solution.py:79
  598.1 1.6 copy.48
  599.7 6.2 gather_fusion.5
  606.0 9.5 %fusion.11 = f32[96,128,128]{2,1,0:T(8,128)} fusion(bf16[96,256,128]{1,2,0:T(8,128)(2,1)} %gather_fusion.5, pred[96]{0:T(512)(128)(4,1)S(1)} %get-tuple-element.8, bf16[96,256,128]{2,1,0:T(8,128)(2,1)} %gather_fusion, pred[96]{0:T(512)(128)(4,1)S(1)} %get-tuple-element.7), kind=kOutput, calls=%fused_computation.19 | convolution fusion | flops 811597824 | bytes 18874560 | tf_op jit(solution)/shard_map/nka,nkq->kaq/dot_general | solution.py:83
  615.4 110.5 %all-reduce.8.cloned.1.call-done = bf16[32,128,256]{2,0,1:T(8,128)(2,1)} async-done(((bf16[32,128,256]{2,0,1:T(8,128)(2,1)}), bf16[32,128,256]{2,0,1:T(8,128)(2,1)}) %all-reduce.8.cloned.1.call-update) | async-done | bytes 2097168 | tf_op jit(solution)/shard_map/psum | solution.py:78
  725.9 4.1 copy.46
  730.0 7.8 %gather_fusion.4 = bf16[96,128,256]{2,1,0:T(8,128)(2,1)} fusion(bf16[32,128,256]{2,1,0:T(8,128)(2,1)} %copy.46, s32[1024]{0:T(1024)S(1)} %pad_clamp_fusion.1), kind=kCustom, calls=%fused_computation.4.clone | custom fusion | bytes 12583296 | tf_op jit(solution)/shard_map/jit(_take)/gather | solution.py:80
  737.8 11.7 %add_multiply_fusion = f32[96,128,128]{2,1,0:T(8,128)} fusion(f32[96,128,128]{2,1,0:T(8,128)} %fusion.11, f32[96]{0:T(128)S(1)} %compare_select_fusion.3, bf16[96,128,256]{2,1,0:T(8,128)(2,1)} %gather_fusion.4, pred[96]{0:T(512)(128)(4,1)S(1)} %get-tuple-element.7, bf16[96,256,128]{2,1,0:T(8,128)(2,1)} %gather_fusion.1, pred[96]{0:T(512)(128)(4,1)S(1)} %get-tuple-element.8), kind=kOutput, calls=%fused_computation.42 | convolution fusion | flops 814743552 | bytes 25166400 | tf_op jit(solution)/shard_map/kan,nkq->kaq/dot_general | solution.py:82
  749.5 10.6 %fusion.10 = f32[1,1,96,128,128]{4,3,2,1,0:T(8,128)} fusion(f32[96,128,128]{2,1,0:T(8,128)S(1)} %bitcast.82, f32[96,128,128]{2,1,0:T(8,128)} %add_multiply_fusion, f32[96]{0:T(128)S(1)} %get-tuple-element.9, pred[128,128]{1,0:T(8,128)(4,1)S(1)} %iota_compare_fusion, pred[96]{0:T(512)(128)(4,1)S(1)} %get-tuple-element.6), kind=kLoop, calls=%fused_computation.18 | loop fusion | flops 22020096 | bytes 18891232 | tf_op jit(solution)/shard_map/reshape | solution.py:90
  (31 shorter events, 0.2 us)
Async XLA Ops:
  7.2 150.9 %all-gather.2.cloned.1.call-start = ((), (), s32[]{:S(2)}) async-start(), calls=%async_computation | async-start | bytes 2228224 | tf_op jit(solution)/shard_map/all_gather | solution.py:44
  120.3 184.2 %all-reduce.12.cloned.1.call-start = ((), (), s32[]{:S(2)}) async-start(), calls=%async_computation.4 | async-start | bytes 4194304 | tf_op jit(solution)/shard_map/psum | solution.py:79
  177.1 6.5 copy-start.2
  196.0 269.2 %all-reduce.6.cloned.1.call-start = ((), (), s32[]{:S(2)}) async-start(), calls=%async_computation.1 | async-start | bytes 4194304 | tf_op jit(solution)/shard_map/psum | solution.py:78
  311.6 11.0 %copy-start.3 = (s32[1,1,96]{2,1,0:T(1,128)S(1)}, s32[1,1,96]{2,1,0:T(1,128)}, u32[]{:S(2)}) copy-start(s32[1,1,96]{2,1,0:T(1,128)} %param.13) | copy-start | bytes 1156
  322.7 17.2 %copy-start.1 = (bf16[256,16,128]{2,1,0:T(8,128)(2,1)S(1)}, bf16[256,16,128]{2,1,0:T(8,128)(2,1)}, u32[]{:S(2)}) copy-start(bf16[256,16,128]{2,1,0:T(8,128)(2,1)} %get-tuple-element.4) | copy-start | bytes 3145732
  339.5 258.6 %all-reduce.10.cloned.1.call-start = ((), (), s32[]{:S(2)}) async-start(), calls=%async_computation.3 | async-start | bytes 2097152 | tf_op jit(solution)/shard_map/psum | solution.py:79
  469.3 20.9 %slice-start = ((s8[6291456]{0:T(1024)(128)(4,1)}), s8[2097152]{0:T(1024)(128)(4,1)S(1)}, s32[]{:S(2)}) async-start(s8[6291456]{0:T(1024)(128)(4,1)} %bitcast.79), calls=%async_computation.5 | async-start | bytes 4194304
  477.1 13.1 %slice-start.1 = ((s8[6291456]{0:T(1024)(128)(4,1)}), s8[4194304]{0:T(1024)(128)(4,1)S(1)}, s32[]{:S(2)}) async-start(s8[6291456]{0:T(1024)(128)(4,1)} %bitcast.79), calls=%async_computation.6 | async-start | bytes 8388608
  490.2 6.4 copy-start
  512.7 213.2 %all-reduce.8.cloned.1.call-start = ((), (), s32[]{:S(2)}) async-start(), calls=%async_computation.2 | async-start | bytes 4194304 | tf_op jit(solution)/shard_map/psum | solution.py:78
  730.0 19.5 %slice-start.2 = ((s8[6291456]{0:T(1024)(128)(4,1)}), s8[2097152]{0:T(1024)(128)(4,1)S(1)}, s32[]{:S(2)}) async-start(s8[6291456]{0:T(1024)(128)(4,1)} %bitcast.81), calls=%async_computation.7 | async-start | bytes 4194304
  737.8 11.7 %slice-start.3 = ((s8[6291456]{0:T(1024)(128)(4,1)}), s8[4194304]{0:T(1024)(128)(4,1)S(1)}, s32[]{:S(2)}) async-start(s8[6291456]{0:T(1024)(128)(4,1)} %bitcast.81), calls=%async_computation.8 | async-start | bytes 8388608
Sparse Core Ops, SparseCore 0:
  120.4 37.6 all-gather.1
  196.1 108.3 all-reduce.11
  339.7 125.4 all-reduce.5
  512.9 85.1 all-reduce.9
  600.5 125.4 all-reduce.7
where the time goes:
time: 771 us; the launch traced here: 767 us
  waiting for transfers between devices  421 us (55%)
  matrix products  144 us (19%)
  blocking collectives  106 us (14%)
  local copies, waits for them, and re-layouts  62.9 us (8%)
  other arithmetic  17.6 us (2%)
  between operations  14.9 us (2%)
    psum x2, waiting for transfers between devices, local(): row_terms = lax.psum(row_part.astype(jnp.bfloat16), 'col')  220 us
    psum x2, waiting for transfers between devices, local(): column_terms = lax.psum(col_part.astype(jnp.bfloat16), 'row')  166 us
    psum x1, blocking collectives, local(): sums = lax.psum(jnp.sum(logged, axis=0), 'col')  53.4 us
    psum x1, blocking collectives, local(): variance = lax.psum(jnp.sum(centered * centered, axis=0), 'col') / samples  52.9 us
    all_gather x1, waiting for transfers between devices, local(): row_x = lax.all_gather(whitened, 'col', axis=0, tiled=True)  35.8 us
    dot_general x2, matrix products, local(): jnp.einsum('tk,kan->tan', row_hot, row_slots, precision=lax.Precision.HIG...  33.7 us
    dot_general x2, matrix products, local(): jnp.einsum('sk,knq->nsq', col_hot, col_slots, precision=lax.Precision.HIG...  28.4 us
    dot_general x2, matrix products, local(): jnp.einsum('kan,nkq->kaq', row_sel, col_pick, preferred_element_type=jnp....  24.8 us
  transfers between devices with their start and end apart: 5, of which 5 were waited for; matrix products, arithmetic and copies ran while one was open for 8% of the time, Pallas kernels for 0%

commit v1 on v0

v1 whole, which is shorter than its diff:
```python
import functools

import jax
import jax.numpy as jnp
from jax import lax
from jax.experimental import pallas as pl
from jax.experimental.pallas import tpu as pltpu
from jax.sharding import PartitionSpec as P

step_size = 0.08
penalty = 1.0
epsilon = 1e-05
MESH = pl.DeviceIdType.MESH
F32 = jnp.float32
BF16 = jnp.bfloat16
GROUP = 8
LIMIT = 40 * 2**20


class Place:
    def __init__(self):
        self.row = lax.axis_index("row")
        self.col = lax.axis_index("col")
        self.y, self.zh = self.row // 2, self.row % 2
        self.zl, self.x, self.core = self.col // 8, (self.col // 2) % 4, self.col % 2
        self.mine = self.core * 8 + self.x * 2 + self.zl
        self.mine_col = self.row

    def at(self, row=None, col=None):
        return (self.row if row is None else row, self.col if col is None else col)

    def xpeer(self, d):
        return self.at(col=self.zl * 8 + ((self.x + d) % 4) * 2 + self.core)

    def ypeer(self, d):
        return self.at(row=((self.y + d) % 4) * 2 + self.zh)

    def zlpeer(self):
        return self.at(col=(1 - self.zl) * 8 + self.x * 2 + self.core)

    def zhpeer(self):
        return self.at(row=self.y * 2 + 1 - self.zh)

    def sibling(self):
        return self.at(col=self.zl * 8 + self.x * 2 + 1 - self.core)


class Wire:
    def __init__(self, send_sem, recv_sem):
        self.send_sem, self.recv_sem = send_sem, recv_sem
        self.copies = {}

    def send(self, name, src, dst, device):
        i = len(self.copies)
        copy = pltpu.make_async_remote_copy(
            src_ref=src, dst_ref=dst, send_sem=self.send_sem.at[i],
            recv_sem=self.recv_sem.at[i], device_id=device, device_id_type=MESH,
        )
        copy.start()
        self.copies[name] = copy

    def recv(self, *names):
        for name in names:
            self.copies[name].wait_recv()

    def drain(self):
        for copy in self.copies.values():
            copy.wait_send()


class Gather:
    def __init__(self, wire, tag, out, base, position, z, ring, zpeer, sibling, done):
        self.w, self.tag, self.out = wire, tag, out
        self.base, self.position, self.z = base, position, z
        self.ring, self.zpeer, self.sibling, self.done = ring, zpeer, sibling, done

    def slot(self, d, other):
        z = 1 - self.z if other else self.z
        return self.base + ((self.position + d) % 4) * 2 + z

    def pass_on(self, name, slot, device):
        self.w.send(self.tag + name, self.out.at[slot], self.out.at[slot], device)

    def have(self, name, slot):
        if self.sibling is not None:
            self.pass_on("core" + name, slot, self.sibling)

    def own(self):
        s = self.slot(0, False)
        self.pass_on("z", s, self.zpeer)
        self.pass_on("own+", s, self.ring(1))
        self.pass_on("own-", s, self.ring(3))
        self.have("own", s)
        self.done(s)

    def other(self):
        s = self.slot(0, True)
        self.w.recv(self.tag + "z")
        self.pass_on("other+", s, self.ring(1))
        self.pass_on("other-", s, self.ring(3))
        self.have("other", s)
        self.done(s)

    def relay(self):
        left, right = self.slot(3, False), self.slot(1, True)
        self.w.recv(self.tag + "own+")
        self.pass_on("far+", left, self.ring(1))
        self.have("a", left)
        self.w.recv(self.tag + "other-")
        self.pass_on("far-", right, self.ring(3))
        self.have("b", right)
        self.done(left)
        self.done(right)

    def near(self):
        left, right = self.slot(3, True), self.slot(1, False)
        self.w.recv(self.tag + "own-")
        self.have("c", right)
        self.w.recv(self.tag + "other+")
        self.have("d", left)
        self.done(right)
        self.done(left)

    def far(self):
        a, b = self.slot(2, False), self.slot(2, True)
        self.w.recv(self.tag + "far+")
        self.have("e", a)
        self.w.recv(self.tag + "far-")
        self.have("f", b)
        self.done(a)
        self.done(b)

    def rest(self):
        if self.sibling is None:
            return
        flip = 8 - 2 * self.base
        for name, d, other in (
            ("own", 0, 0), ("other", 0, 1), ("a", 3, 0), ("b", 1, 1),
            ("c", 1, 0), ("d", 3, 1), ("e", 2, 0), ("f", 2, 1),
        ):
            self.w.recv(self.tag + "core" + name)
            self.done(self.slot(d, other) + flip)


def row_gather(wire, place, out, done):
    return Gather(wire, "r", out, place.core * 8, place.x, place.zl, place.xpeer, place.zlpeer(), place.sibling(), done)


def col_gather(wire, place, out, done):
    return Gather(wire, "c", out, 0, place.y, place.zh, place.ypeer, place.zhpeer(), None, done)


def greet(devices):
    barrier = pltpu.get_barrier_semaphore()
    for device in devices:
        pl.semaphore_signal(barrier, inc=1, device_id=device, device_id_type=MESH)
    return barrier


def prep_kernel(counts, whiten, xr, xc, xrt, xct, packed, landed, wbuf, wsem, lsem, send_sem, recv_sem):
    place = Place()
    block, half = place.mine // 2, place.mine % 2
    to_row, to_col = place.x * 2 + place.zl, 2 * place.row + place.core
    from_row, from_col = place.col // 2, (place.row % 2) * 8 + (place.row // 2) * 2 + place.core
    moves = jnp.logical_or(to_row != place.row, to_col != place.col)
    peers = [place.at(col=(place.col + d) % 16) for d in range(1, 16)]
    peers += [place.ypeer(d) for d in (1, 3)] + [place.zhpeer()]
    barrier = greet(peers)

    @pl.when(moves)
    def _():
        for device in ((to_row, to_col), (from_row, from_col)):
            pl.semaphore_signal(barrier, inc=1, device_id=device, device_id_type=MESH)

    load = pltpu.make_async_copy(
        whiten.at[block, :, pl.ds(pl.multiple_of(half * 256, 256), 256)], wbuf, wsem
    )
    load.start()
    for b in range(8):
        packed[b] = counts[:, b * 512 : (b + 1) * 512].astype(jnp.int16)
    pl.semaphore_wait(barrier, len(peers) + 2 * moves.astype(jnp.int32))

    wire = Wire(send_sem, recv_sem)
    for d in range(1, 16):
        c = (place.col + d) % 16
        b = (c % 2) * 4 + (c // 2) % 4
        wire.send(f"a{d}", packed.at[b], landed.at[place.col], place.at(col=c))
    landed[place.col] = packed[block]
    wire.recv(*[f"a{d}" for d in range(1, 16)])
    load.wait()
    logged = jnp.log(1.0 + landed[...].astype(jnp.int32).astype(F32)).reshape(256, 512)
    mean = jnp.mean(logged, axis=0, keepdims=True)
    centered = logged - mean
    variance = jnp.mean(centered * centered, axis=0, keepdims=True)
    standard = (centered * lax.rsqrt(variance + epsilon)).astype(BF16)
    whitened = jnp.dot(standard, wbuf[...], preferred_element_type=F32).astype(BF16)
    xr[place.mine, :256] = whitened[:, :128]
    xr[place.mine, 256:] = whitened[:, 128:]

    def turn(source, target):
        def done(s):
            target[s, :128] = source[s, :256].T
            target[s, 128:] = source[s, 256:].T

        return done

    row = row_gather(wire, place, xr, turn(xr, xrt))
    col = col_gather(wire, place, xc, turn(xc, xct))
    hop = pltpu.make_async_remote_copy(
        src_ref=xr.at[place.mine], dst_ref=xc.at[to_row], send_sem=lsem.at[0],
        recv_sem=lsem.at[1], device_id=(to_row, to_col), device_id_type=MESH,
    )

    @pl.when(moves)
    def _():
        hop.start()

    @pl.when(jnp.logical_not(moves))
    def _():
        xc[place.mine_col] = xr[place.mine]

    row.own()

    @pl.when(moves)
    def _():
        hop.wait_recv()

    col.own()
    row.other()
    col.other()
    row.relay()
    col.relay()
    row.near()
    col.near()
    row.far()
    col.far()
    row.rest()
    wire.drain()

    @pl.when(moves)
    def _():
        hop.wait_send()


def add(*parts):
    total = parts[0].astype(F32)
    for part in parts[1:]:
        total = total + part.astype(F32)
    return total


class Scatter:
    def __init__(self, wire, tag, land, zland, keep, zout, z, ring, zpeer, pick, stage):
        self.w, self.tag, self.land, self.zland = wire, tag, land, zland
        self.keep, self.zout, self.z = keep, zout, z
        self.ring, self.zpeer, self.pick, self.stage = ring, zpeer, pick, stage

    def put(self, name, i, src, device):
        self.w.send(self.tag + name, src, self.land.at[i], device)

    def first(self):
        self.put("A1", 0, self.stage(2, 0), self.ring(1))
        self.put("B1", 1, self.stage(2, 1), self.ring(3))

    def second(self):
        self.put("A2", 2, self.stage(1, 1), self.ring(1))
        self.put("B2", 3, self.stage(3, 0), self.ring(3))

    def merge(self):
        self.w.recv(self.tag + "A1")
        self.land[0] = add(self.pick(1, 0), self.land[0]).astype(BF16)
        self.put("A3", 4, self.land.at[0], self.ring(1))
        self.w.recv(self.tag + "B1")
        self.land[1] = add(self.pick(3, 1), self.land[1]).astype(BF16)
        self.put("B3", 5, self.land.at[1], self.ring(3))

    def cross(self):
        self.w.recv(*[self.tag + n for n in ("B2", "A2", "A3", "B3")])
        own = (add(self.pick(0, 0), self.land[3], self.land[4]), add(self.pick(0, 1), self.land[2], self.land[5]))
        mine = self.z == 0
        self.zout[...] = jnp.where(mine, own[1], own[0]).astype(BF16)
        self.w.send(self.tag + "Z", self.zout, self.zland, self.zpeer)
        self.keep[...] = jnp.where(mine, own[0], own[1])

    def last(self, out, slot):
        self.w.recv(self.tag + "Z")
        out[slot] = add(self.keep[...], self.zland[...]).astype(BF16)


def reduce_kernel(
    rp, cp, u, v, pair, summed, rland, rzland, rkeep, rzout, cland, czland, ckeep, czout, send_sem, recv_sem
):
    place = Place()
    peers = [place.sibling(), place.xpeer(1), place.xpeer(3), place.zlpeer()]
    peers += [place.ypeer(1), place.ypeer(3), place.zhpeer()]
    barrier = greet(peers)
    pl.semaphore_wait(barrier, len(peers))
    wire = Wire(send_sem, recv_sem)
    here, there = place.core * 8, 8 - place.core * 8

    def rslot(d, e):
        return ((place.x + d) % 4) * 2 + e

    def cslot(d, e):
        return ((place.y + d) % 4) * 2 + e

    order = ((2, 0), (2, 1), (1, 1), (3, 0), (1, 0), (3, 1), (0, 0), (0, 1))
    for d, e in order:
        s = rslot(d, e)
        wire.send(f"s{d}{e}", rp.at[there + s], pair.at[s], place.sibling())
    col = Scatter(
        wire, "cs", cland, czland, ckeep, czout, place.zh, place.ypeer, place.zhpeer(),
        lambda d, e: cp[cslot(d, e)], lambda d, e: cp.at[cslot(d, e)],
    )
    row = Scatter(
        wire, "rs", rland, rzland, rkeep, rzout, place.zl, place.xpeer, place.zlpeer(),
        lambda d, e: summed[rslot(d, e)], lambda d, e: summed.at[rslot(d, e)],
    )
    col.first()
    col.second()

    def join(d, e):
        s = rslot(d, e)
        wire.recv(f"s{d}{e}")
        summed[s] = add(rp[here + s], pair[s]).astype(BF16)

    for d, e in order[:2]:
        join(d, e)
    row.first()
    for d, e in order[2:4]:
        join(d, e)
    row.second()
    for d, e in order[4:]:
        join(d, e)
    col.merge()
    row.merge()
    col.cross()
    row.cross()
    nothing = lambda s: None
    rg = row_gather(wire, place, u, nothing)
    cg = col_gather(wire, place, v, nothing)
    col.last(v, place.mine_col)
    cg.own()
    row.last(u, place.mine)
    rg.own()
    cg.other()
    rg.other()
    cg.relay()
    rg.relay()
    cg.near()
    rg.near()
    cg.far()
    rg.far()
    rg.rest()
    wire.drain()


def tile_kernel(first, last, *refs):
    refs = list(refs)
    rows, cols, count, where_at, tiles = refs[:5]
    refs = refs[5:]
    if not first:
        u, v, xrt, xc = refs[:4]
        refs = refs[4:]
    if not last:
        xr, xct = refs[:2]
        refs = refs[2:]
    if not first:
        omega_out = refs.pop(0)
    if last:
        grad_out = refs.pop(0)
    else:
        rp, cp, racc, cacc = refs
    step = pl.program_id(0)
    live = count[0]

    if not last:

        @pl.when(step == 0)
        def _():
            racc[...] = jnp.zeros_like(racc)
            cacc[...] = jnp.zeros_like(cacc)

    @pl.when(step * GROUP < live)
    def _():
        if not first:
            identity = lax.broadcasted_iota(jnp.int32, (128, 128), 0) == lax.broadcasted_iota(jnp.int32, (128, 128), 1)
        for j in range(GROUP):
            k = step * GROUP + j
            alive = k < live
            sr, sc = rows[k], cols[k]
            omega = jnp.where(alive, tiles[j], 0.0)
            if not first:
                left = jnp.dot(u[sr], xc[sc], preferred_element_type=F32)
                right = jnp.dot(xrt[sr], v[sc], preferred_element_type=F32)
                grad = jnp.where(alive, (left + right) * (0.5 / 256), 0.0)
                moved = omega - step_size * grad
                t = step_size * penalty
                shrunk = moved - jnp.clip(moved, -t, t)
                diagonal = 0.5 * (moved + jnp.sqrt(moved * moved + 4.0 * step_size))
                on = jnp.logical_and(identity, jnp.logical_and(alive, where_at[0] + sr == where_at[1] + sc))
                omega = jnp.where(on, diagonal, shrunk)
                omega_out[j] = omega
                if last:
                    grad_out[j] = grad
            if not last:
                low = omega.astype(BF16)
                racc[sr] += jnp.dot(low, xct[sc], preferred_element_type=F32)
                cacc[sc] += jnp.dot(xr[sr], low, preferred_element_type=F32)

    if not first:

        @pl.when(step * GROUP >= live)
        def _():
            omega_out[...] = jnp.zeros_like(omega_out)
            if last:
                grad_out[...] = jnp.zeros_like(grad_out)

    if not last:

        @pl.when(step == pl.num_programs(0) - 1)
        def _():
            rp[...] = racc[...].astype(BF16)
            cp[...] = cacc[...].astype(BF16)


def tile_call(first, last, scalars, tiles, dense):
    slots = tiles.shape[0]
    smem = pl.BlockSpec(memory_space=pltpu.SMEM)
    vmem = pl.BlockSpec(memory_space=pltpu.VMEM)
    block = pl.BlockSpec((GROUP, 128, 128), lambda i: (i, 0, 0))
    out_shape, out_specs, scratch = [], [], []
    if not first:
        out_shape.append(jax.ShapeDtypeStruct(tiles.shape, F32))
        out_specs.append(block)
    if last:
        out_shape.append(jax.ShapeDtypeStruct(tiles.shape, F32))
        out_specs.append(block)
    else:
        out_shape += [jax.ShapeDtypeStruct((32, 128, 256), BF16), jax.ShapeDtypeStruct((16, 256, 128), BF16)]
        out_specs += [vmem, vmem]
        scratch = [pltpu.VMEM((32, 128, 256), F32), pltpu.VMEM((16, 256, 128), F32)]
    return pl.pallas_call(
        functools.partial(tile_kernel, first, last),
        grid=(slots // GROUP,),
        out_shape=out_shape,
        in_specs=[smem] * 4 + [block] + [vmem] * len(dense),
        out_specs=out_specs,
        scratch_shapes=scratch,
        compiler_params=pltpu.CompilerParams(vmem_limit_bytes=LIMIT),
    )(*scalars, tiles, *dense)


def prep(counts, whiten):
    vmem = pl.BlockSpec(memory_space=pltpu.VMEM)
    n = 15 + 15 + 7
    shapes = ((16, 512, 128), (8, 512, 128), (16, 256, 256), (8, 256, 256))
    return pl.pallas_call(
        prep_kernel,
        out_shape=[jax.ShapeDtypeStruct(s, BF16) for s in shapes],
        in_specs=[vmem, pl.BlockSpec(memory_space=pl.ANY)],
        out_specs=[vmem] * 4,
        scratch_shapes=[
            pltpu.VMEM((8, 16, 512), jnp.int16),
            pltpu.VMEM((16, 16, 512), jnp.int16),
            pltpu.VMEM((512, 256), BF16),
            pltpu.SemaphoreType.DMA,
            pltpu.SemaphoreType.DMA((2,)),
            pltpu.SemaphoreType.DMA((n,)),
            pltpu.SemaphoreType.DMA((n,)),
        ],
        compiler_params=pltpu.CompilerParams(collective_id=0, has_side_effects=True, vmem_limit_bytes=LIMIT),
    )(counts, whiten)


def reduce_both(rp, cp, collective_id):
    vmem = pl.BlockSpec(memory_space=pltpu.VMEM)
    n = 8 + 7 + 7 + 15 + 7
    u, v = pl.pallas_call(
        reduce_kernel,
        out_shape=[jax.ShapeDtypeStruct((16, 256, 256), BF16), jax.ShapeDtypeStruct((8, 512, 128), BF16)],
        in_specs=[vmem] * 2,
        out_specs=[vmem] * 2,
        scratch_shapes=[
            pltpu.VMEM((8, 256, 256), BF16),
            pltpu.VMEM((8, 256, 256), BF16),
            pltpu.VMEM((6, 256, 256), BF16),
            pltpu.VMEM((256, 256), BF16),
            pltpu.VMEM((256, 256), F32),
            pltpu.VMEM((256, 256), BF16),
            pltpu.VMEM((6, 512, 128), BF16),
            pltpu.VMEM((512, 128), BF16),
            pltpu.VMEM((512, 128), F32),
            pltpu.VMEM((512, 128), BF16),
            pltpu.SemaphoreType.DMA((n,)),
            pltpu.SemaphoreType.DMA((n,)),
        ],
        compiler_params=pltpu.CompilerParams(
            collective_id=collective_id, has_side_effects=True, vmem_limit_bytes=LIMIT
        ),
    )(rp.reshape(16, 256, 256), cp.reshape(8, 512, 128))
    return u.reshape(32, 128, 256), v.reshape(16, 256, 128)


def local(counts, whiten, initial_tiles, tile_rows, tile_cols, tile_count):
    tiles = initial_tiles.reshape(96, 128, 128)
    where_at = jnp.stack([lax.axis_index("row") * 32, lax.axis_index("col") * 16]).astype(jnp.int32)
    scalars = (tile_rows.reshape(96), tile_cols.reshape(96), tile_count.reshape(1), where_at)
    xr, xc, xrt, xct = prep(counts, whiten)
    xr, xc = xr.reshape(32, 256, 128), xc.reshape(16, 256, 128)
    xrt, xct = xrt.reshape(32, 128, 256), xct.reshape(16, 128, 256)
    rp, cp = tile_call(True, False, scalars, tiles, (xr, xct))
    u, v = reduce_both(rp, cp, 1)
    omega, rp, cp = tile_call(False, False, scalars, tiles, (u, v, xrt, xc, xr, xct))
    u, v = reduce_both(rp, cp, 2)
    omega, grad = tile_call(False, True, scalars, omega, (u, v, xrt, xc))
    return omega.reshape(initial_tiles.shape), grad.reshape(initial_tiles.shape)


def solution(mesh):
    in_specs = (
        P("col", "row"),
        P("row", None, None),
        P("row", "col", None, None, None),
        P("row", "col", None),
        P("row", "col", None),
        P("row", "col"),
    )
    out_specs = (P("row", "col", None, None, None), P("row", "col", None, None, None))
    return jax.shard_map(local, mesh=mesh, in_specs=in_specs, out_specs=out_specs, check_vma=False)
```

time: 771 us -> 156 us (0.20)
  waiting for transfers between devices: 421 us -> 0 us
  Pallas kernels: 0 us -> 145 us
  matrix products: 144 us -> 0 us
  blocking collectives: 106 us -> 0 us
  local copies, waits for them, and re-layouts: 62.9 us -> 8.7 us
  other arithmetic: 17.6 us -> 0.08 us
  between operations: 14.9 us -> 1.35 us
    psum x4 -> x0, waiting for transfers between devices: 385 us -> none  [the longest x2 220 us: local(): row_terms = lax.psum(row_part.astype(jnp.bfloat16), 'col')]
    pallas_call x0 -> x6, Pallas kernels: none -> 145 us  [the longest x2 81.8 us: reduce_both(): pl.pallas_call(reduce_kernel, out_shape=[jax.ShapeDtypeStruct((16, 256, 2...]
    dot_general x13 -> x0, matrix products: 144 us -> none  [the longest x2 33.7 us: local(): jnp.einsum('tk,kan->tan', row_hot, row_slots, precision=lax.Precision.HIG...]
    psum x2 -> x0, blocking collectives: 106 us -> none  [the longest x1 53.4 us: local(): sums = lax.psum(jnp.sum(logged, axis=0), 'col')]
    gather x6 -> x0, local copies, waits for them, and re-layouts: 41.5 us -> none  [the longest x2 15.6 us: local(): row_sel = jnp.take(row_terms, slot_rows, axis=0)]
    all_gather x1 -> x0, waiting for transfers between devices: 35.8 us -> none  [local(): row_x = lax.all_gather(whitened, 'col', axis=0, tiled=True)]
    psum x4 -> x0, local copies, waits for them, and re-layouts: 10.6 us -> none  [the longest x2 8.2 us: local(): row_terms = lax.psum(row_part.astype(jnp.bfloat16), 'col')]
    reshape x1 -> x0, other arithmetic: 10.6 us -> none  [local(): return (omega.reshape(out_shape), gradient.reshape(out_shape))]
  transfers between devices with their start and end apart: 5 -> 0, of which waited for: 5 -> 0; matrix products, arithmetic and copies ran while one was open for 8% -> 0% of each run, Pallas kernels for 0% -> 0%
where the time goes in v1:
time: 156 us; the launch traced here: 155 us
  Pallas kernels  145 us (93%)
  local copies, waits for them, and re-layouts  8.7 us (6%)
    pallas_call x2, Pallas kernels, reduce_both(): pl.pallas_call(reduce_kernel, out_shape=[jax.ShapeDtypeStruct((16, 256, 2...  81.8 us
    pallas_call x1, Pallas kernels, prep(): pl.pallas_call(prep_kernel, out_shape=[jax.ShapeDtypeStruct(s, BF16) for...  34.8 us
    pallas_call x3, Pallas kernels, tile_call(): pl.pallas_call(functools.partial(tile_kernel, first, last), grid=(slots /...  27.9 us
    unnamed x12, local copies, waits for them, and re-layouts  8.7 us

profile of v1, /device:TPU:1, one launch (start us, length us, event | category | flops | bytes accessed | tf_op | source)
XLA Modules:
  0.0 154.7 jit_solution(8810487142759739174)
XLA Ops:
  1.3 0.1 pad_add_fusion.refs_3_
  1.4 0.0 copy-start.2
  1.4 2.2 %copy-done.2 = bf16[8,512,512]{2,1,0:T(8,128)(2,1)S(1)} copy-done((bf16[8,512,512]{2,1,0:T(8,128)(2,1)S(1)}, bf16[8,512,512]{2,1,0:T(8,128)(2,1)}, u32[]{:S(2)}) %copy-start.2) | copy-done | bytes 4194328
  3.5 0.0 copy-start.3
  3.5 0.9 copy-done.3
  4.5 0.0 copy-start.4
  4.5 0.0 copy-start.5
  4.5 34.8 %shard_map.77 = (bf16[16,512,128]{2,1,0:T(8,128)(2,1)S(1)}, bf16[8,512,128]{2,1,0:T(8,128)(2,1)S(1)}, bf16[16,256,256]{2,1,0:T(8,128)(2,1)S(1)}, bf16[8,256,256]{2,1,0:T(8,128)(2,1)S(1)}) custom-call(s32[16,4096]{1,0:T(8,128)S(1)} %copy-done.3, bf16[8,512,512]{2,1,0:T(8,128)(2,1)S(1)} %copy-done.2), custom_call_target="tpu_custom_call" | custom-call | tf_op jit(solution)/shard_map/pallas_call | solution.py:458
  39.4 0.0 copy-done.4
  39.4 0.0 copy-done.5
  39.4 0.0 copy-start
  39.4 2.8 %copy-done = f32[1,1,96,128,128]{4,3,2,1,0:T(8,128)S(1)} copy-done((f32[1,1,96,128,128]{4,3,2,1,0:T(8,128)S(1)}, f32[1,1,96,128,128]{4,3,2,1,0:T(8,128)}, u32[]{:S(2)}) %copy-start) | copy-done | bytes 6291480
  42.2 3.5 %shard_map.78 = (bf16[32,128,256]{2,1,0:T(8,128)(2,1)S(1)}, bf16[16,256,128]{2,1,0:T(8,128)(2,1)S(1)}) custom-call(s32[96]{0:T(128)S(1)} %bitcast.41, s32[96]{0:T(128)S(1)} %bitcast.44, s32[1]{0:T(128)} %bitcast.20.refs_2_, s32[2]{0:T(128)S(1)} %pad_add_fusion.refs_3_, f32[96,128,128]{2,1,0:T(8,128)S(1)} %bitcast.24, bf16[32,256,128]{2,1,0:T(8,128)(2,1)S(1)} %bitcast.25, ...), custom_call_target="tpu_custom_call" | custom-call | tf_op jit(solution)/shard_map/pallas_call | solution.py:443
  45.7 41.2 %shard_map.79 = (bf16[16,256,256]{2,1,0:T(8,128)(2,1)S(1)}, bf16[8,512,128]{2,1,0:T(8,128)(2,1)S(1)}) custom-call(bf16[16,256,256]{2,1,0:T(8,128)(2,1)S(1)} %bitcast.35, bf16[8,512,128]{2,1,0:T(8,128)(2,1)S(1)} %bitcast.39), custom_call_target="tpu_custom_call" | custom-call | tf_op jit(solution)/shard_map/pallas_call | solution.py:479
  86.9 15.7 %shard_map.80 = (f32[96,128,128]{2,1,0:T(8,128)}, bf16[32,128,256]{2,1,0:T(8,128)(2,1)S(1)}, bf16[16,256,128]{2,1,0:T(8,128)(2,1)S(1)}) custom-call(s32[96]{0:T(128)S(1)} %bitcast.42, s32[96]{0:T(128)S(1)} %bitcast.45, s32[1]{0:T(128)} %bitcast.21.refs_2_, s32[2]{0:T(128)S(1)} %pad_add_fusion.refs_3_, f32[96,128,128]{2,1,0:T(8,128)} %bitcast.23, ...), custom_call_target="tpu_custom_call" | custom-call | tf_op jit(solution)/shard_map/pallas_call | solution.py:443
  102.7 40.6 %shard_map.81 = (bf16[16,256,256]{2,1,0:T(8,128)(2,1)S(1)}, bf16[8,512,128]{2,1,0:T(8,128)(2,1)S(1)}) custom-call(bf16[16,256,256]{2,1,0:T(8,128)(2,1)S(1)} %bitcast.34, bf16[8,512,128]{2,1,0:T(8,128)(2,1)S(1)} %bitcast.38), custom_call_target="tpu_custom_call" | custom-call | tf_op jit(solution)/shard_map/pallas_call | solution.py:479
  143.3 0.0 copy-start.1
  143.3 2.8 %copy-done.1 = f32[96,128,128]{2,1,0:T(8,128)S(1)} copy-done((f32[96,128,128]{2,1,0:T(8,128)S(1)}, f32[96,128,128]{2,1,0:T(8,128)}, u32[]{:S(2)}) %copy-start.1) | copy-done | bytes 6291480
  146.0 8.6 %shard_map.82 = (f32[96,128,128]{2,1,0:T(8,128)}, f32[96,128,128]{2,1,0:T(8,128)}) custom-call(s32[96]{0:T(128)S(1)} %bitcast.43, s32[96]{0:T(128)S(1)} %bitcast.46, s32[1]{0:T(128)} %bitcast.22.refs_2_, s32[2]{0:T(128)S(1)} %pad_add_fusion.refs_3_, f32[96,128,128]{2,1,0:T(8,128)S(1)} %copy-done.1, bf16[32,128,256]{2,1,0:T(8,128)(2,1)S(1)} %bitcast.36, ...), custom_call_target="tpu_custom_call" | custom-call | tf_op jit(solution)/shard_map/pallas_call | solution.py:443
Async XLA Ops:
  1.4 2.2 %copy-start.2 = (bf16[8,512,512]{2,1,0:T(8,128)(2,1)S(1)}, bf16[8,512,512]{2,1,0:T(8,128)(2,1)}, u32[]{:S(2)}) copy-start(bf16[8,512,512]{2,1,0:T(8,128)(2,1)} %whiten.1) | copy-start | bytes 12582916
  3.5 0.9 copy-start.3
  4.5 34.9 %copy-start.4 = (s32[1,1,96]{2,1,0:T(1,128)S(1)}, s32[1,1,96]{2,1,0:T(1,128)}, u32[]{:S(2)}) copy-start(s32[1,1,96]{2,1,0:T(1,128)} %param.9) | copy-start | bytes 1156
  4.5 34.9 %copy-start.5 = (s32[1,1,96]{2,1,0:T(1,128)S(1)}, s32[1,1,96]{2,1,0:T(1,128)}, u32[]{:S(2)}) copy-start(s32[1,1,96]{2,1,0:T(1,128)} %param.10) | copy-start | bytes 1156
  39.4 2.8 %copy-start = (f32[1,1,96,128,128]{4,3,2,1,0:T(8,128)S(1)}, f32[1,1,96,128,128]{4,3,2,1,0:T(8,128)}, u32[]{:S(2)}) copy-start(f32[1,1,96,128,128]{4,3,2,1,0:T(8,128)} %param.8) | copy-start | bytes 18874372
  143.3 2.8 %copy-start.1 = (f32[96,128,128]{2,1,0:T(8,128)S(1)}, f32[96,128,128]{2,1,0:T(8,128)}, u32[]{:S(2)}) copy-start(f32[96,128,128]{2,1,0:T(8,128)} %get-tuple-element.25.refs_4_) | copy-start | bytes 18874372

commit v2 on v1

--- a/solution.py
+++ b/solution.py
@@ -14,7 +14,8 @@
 F32 = jnp.float32
 BF16 = jnp.bfloat16
 GROUP = 8
-LIMIT = 40 * 2**20
+MIB = 2**20
+PREP_MIB = 39
 
 
 class Place:
@@ -157,9 +158,11 @@
     return barrier
 
 
-def prep_kernel(counts, whiten, xr, xc, xrt, xct, packed, landed, wbuf, wsem, lsem, send_sem, recv_sem):
+def prep_kernel(
+    counts_hbm, tiles_hbm, whiten, xr, xc, xrt, xct, tiles, counts, packed, landed, wsem, lsem, send_sem, recv_sem
+):
     place = Place()
-    block, half = place.mine // 2, place.mine % 2
+    block = place.mine // 2
     to_row, to_col = place.x * 2 + place.zl, 2 * place.row + place.core
     from_row, from_col = place.col // 2, (place.row % 2) * 8 + (place.row // 2) * 2 + place.core
     moves = jnp.logical_or(to_row != place.row, to_col != place.col)
@@ -172,10 +175,11 @@
         for device in ((to_row, to_col), (from_row, from_col)):
             pl.semaphore_signal(barrier, inc=1, device_id=device, device_id_type=MESH)
 
-    load = pltpu.make_async_copy(
-        whiten.at[block, :, pl.ds(pl.multiple_of(half * 256, 256), 256)], wbuf, wsem
-    )
-    load.start()
+    counted = pltpu.make_async_copy(counts_hbm, counts, wsem.at[0])
+    tiled = pltpu.make_async_copy(tiles_hbm, tiles, wsem.at[1])
+    counted.start()
+    tiled.start()
+    counted.wait()
     for b in range(8):
         packed[b] = counts[:, b * 512 : (b + 1) * 512].astype(jnp.int16)
     pl.semaphore_wait(barrier, len(peers) + 2 * moves.astype(jnp.int32))
@@ -187,13 +191,12 @@
         wire.send(f"a{d}", packed.at[b], landed.at[place.col], place.at(col=c))
     landed[place.col] = packed[block]
     wire.recv(*[f"a{d}" for d in range(1, 16)])
-    load.wait()
     logged = jnp.log(1.0 + landed[...].astype(jnp.int32).astype(F32)).reshape(256, 512)
     mean = jnp.mean(logged, axis=0, keepdims=True)
     centered = logged - mean
     variance = jnp.mean(centered * centered, axis=0, keepdims=True)
     standard = (centered * lax.rsqrt(variance + epsilon)).astype(BF16)
-    whitened = jnp.dot(standard, wbuf[...], preferred_element_type=F32).astype(BF16)
+    whitened = jnp.dot(standard, whiten[...], preferred_element_type=F32).astype(BF16)
     xr[place.mine, :256] = whitened[:, :128]
     xr[place.mine, 256:] = whitened[:, 128:]
 
@@ -235,6 +238,7 @@
     row.far()
     col.far()
     row.rest()
+    tiled.wait()
     wire.drain()
 
     @pl.when(moves)
@@ -355,122 +359,156 @@
     wire.drain()
 
 
-def tile_kernel(first, last, *refs):
-    refs = list(refs)
-    rows, cols, count, where_at, tiles = refs[:5]
-    refs = refs[5:]
-    if not first:
-        u, v, xrt, xc = refs[:4]
-        refs = refs[4:]
-    if not last:
-        xr, xct = refs[:2]
-        refs = refs[2:]
-    if not first:
-        omega_out = refs.pop(0)
-    if last:
-        grad_out = refs.pop(0)
-    else:
-        rp, cp, racc, cacc = refs
-    step = pl.program_id(0)
+def live_groups(count):
+    return (count[0] + GROUP - 1) // GROUP
+
+
+def gradient(k, live, rows, cols, u, v, xrt, xc):
+    sr, sc = rows[k], cols[k]
+    left = jnp.dot(u[sr], xc[sc], preferred_element_type=F32)
+    right = jnp.dot(xrt[sr], v[sc], preferred_element_type=F32)
+    return jnp.where(k < live, (left + right) * (0.5 / 256), 0.0)
+
+
+def moved_to(k, live, rows, cols, where_at, identity, omega, grad):
+    moved = omega - step_size * grad
+    t = step_size * penalty
+    shrunk = moved - jnp.clip(moved, -t, t)
+    diagonal = 0.5 * (moved + jnp.sqrt(moved * moved + 4.0 * step_size))
+    on = jnp.logical_and(k < live, where_at[0] + rows[k] == where_at[1] + cols[k])
+    return jnp.where(jnp.logical_and(identity, on), diagonal, shrunk)
+
+
+def eye():
+    return lax.broadcasted_iota(jnp.int32, (128, 128), 0) == lax.broadcasted_iota(jnp.int32, (128, 128), 1)
+
+
+def products(k, low, rows, cols, xr, xct, racc, cacc):
+    sr, sc = rows[k], cols[k]
+    racc[sr] += jnp.dot(low, xct[sc], preferred_element_type=F32)
+    cacc[sc] += jnp.dot(xr[sr], low, preferred_element_type=F32)
+
+
+def first_kernel(rows, cols, count, where_at, tiles, xr, xct, rp, cp, racc, cacc):
+    racc[...] = jnp.zeros_like(racc)
+    cacc[...] = jnp.zeros_like(cacc)
     live = count[0]
 
-    if not last:
-
-        @pl.when(step == 0)
-        def _():
-            racc[...] = jnp.zeros_like(racc)
-            cacc[...] = jnp.zeros_like(cacc)
-
-    @pl.when(step * GROUP < live)
-    def _():
-        if not first:
-            identity = lax.broadcasted_iota(jnp.int32, (128, 128), 0) == lax.broadcasted_iota(jnp.int32, (128, 128), 1)
+    def group(g, _):
         for j in range(GROUP):
-            k = step * GROUP + j
-            alive = k < live
-            sr, sc = rows[k], cols[k]
-            omega = jnp.where(alive, tiles[j], 0.0)
-            if not first:
-                left = jnp.dot(u[sr], xc[sc], preferred_element_type=F32)
-                right = jnp.dot(xrt[sr], v[sc], preferred_element_type=F32)
-                grad = jnp.where(alive, (left + right) * (0.5 / 256), 0.0)
-                moved = omega - step_size * grad
-                t = step_size * penalty
-                shrunk = moved - jnp.clip(moved, -t, t)
-                diagonal = 0.5 * (moved + jnp.sqrt(moved * moved + 4.0 * step_size))
-                on = jnp.logical_and(identity, jnp.logical_and(alive, where_at[0] + sr == where_at[1] + sc))
-                omega = jnp.where(on, diagonal, shrunk)
-                omega_out[j] = omega
-                if last:
-                    grad_out[j] = grad
-            if not last:
-                low = omega.astype(BF16)
-                racc[sr] += jnp.dot(low, xct[sc], preferred_element_type=F32)
-                cacc[sc] += jnp.dot(xr[sr], low, preferred_element_type=F32)
-
-    if not first:
-
-        @pl.when(step * GROUP >= live)
-        def _():
-            omega_out[...] = jnp.zeros_like(omega_out)
-            if last:
-                grad_out[...] = jnp.zeros_like(grad_out)
-
-    if not last:
-
-        @pl.when(step == pl.num_programs(0) - 1)
-        def _():
-            rp[...] = racc[...].astype(BF16)
-            cp[...] = cacc[...].astype(BF16)
-
-
-def tile_call(first, last, scalars, tiles, dense):
-    slots = tiles.shape[0]
+            k = g * GROUP + j
+            low = jnp.where(k < live, tiles[k], 0.0).astype(BF16)
+            products(k, low, rows, cols, xr, xct, racc, cacc)
+        return 0
+
+    lax.fori_loop(0, live_groups(count), group, 0)
+    rp[...] = racc[...].astype(BF16)
+    cp[...] = cacc[...].astype(BF16)
+
+
+def middle_kernel(
+    rows, cols, count, where_at, tiles, u, v, xrt, xc, xr, xct, omega_out, rp, cp, racc, cacc, low
+):
+    racc[...] = jnp.zeros_like(racc)
+    cacc[...] = jnp.zeros_like(cacc)
+    live = count[0]
+
+    def group(g, _):
+        identity = eye()
+        for j in range(GROUP):
+            k = g * GROUP + j
+            grad = gradient(k, live, rows, cols, u, v, xrt, xc)
+            omega = jnp.where(k < live, tiles[k], 0.0)
+            omega = moved_to(k, live, rows, cols, where_at, identity, omega, grad)
+            omega_out[k] = omega
+            low[j] = omega.astype(BF16)
+        for j in range(GROUP):
+            products(g * GROUP + j, low[j], rows, cols, xr, xct, racc, cacc)
+        return 0
+
+    lax.fori_loop(0, live_groups(count), group, 0)
+    rp[...] = racc[...].astype(BF16)
+    cp[...] = cacc[...].astype(BF16)
+
+
+def last_kernel(rows, cols, count, where_at, tiles, u, v, xrt, xc, omega_out, grad_out, obuf, gbuf, zeros, sem):
+    live = count[0]
+    groups, total = live_groups(count), omega_out.shape[0] // GROUP
+
+    def writes(g, o, d):
+        here = pl.ds(g * GROUP, GROUP)
+        return (
+            pltpu.make_async_copy(o, omega_out.at[here], sem.at[0, g]),
+            pltpu.make_async_copy(d, grad_out.at[here], sem.at[1, g]),
+        )
+
+    zeros[...] = jnp.zeros_like(zeros)
+
+    def dead(g, _):
+        for copy in writes(g, zeros, zeros):
+            copy.start()
+        return 0
+
+    lax.fori_loop(groups, total, dead, 0)
+
+    def group(g, _):
+        identity = eye()
+        for j in range(GROUP):
+            k = g * GROUP + j
+            grad = gradient(k, live, rows, cols, u, v, xrt, xc)
+            omega = jnp.where(k < live, tiles[k], 0.0)
+            gbuf[k] = grad
+            obuf[k] = moved_to(k, live, rows, cols, where_at, identity, omega, grad)
+        here = pl.ds(g * GROUP, GROUP)
+        for copy in writes(g, obuf.at[here], gbuf.at[here]):
+            copy.start()
+        return 0
+
+    lax.fori_loop(0, groups, group, 0)
+
+    def wait(g, _):
+        for copy in writes(g, zeros, zeros):
+            copy.wait()
+        return 0
+
+    lax.fori_loop(0, total, wait, 0)
+
+
+def tile_call(kernel, scalars, dense, out_shape, out_space, scratch, limit):
     smem = pl.BlockSpec(memory_space=pltpu.SMEM)
     vmem = pl.BlockSpec(memory_space=pltpu.VMEM)
-    block = pl.BlockSpec((GROUP, 128, 128), lambda i: (i, 0, 0))
-    out_shape, out_specs, scratch = [], [], []
-    if not first:
-        out_shape.append(jax.ShapeDtypeStruct(tiles.shape, F32))
-        out_specs.append(block)
-    if last:
-        out_shape.append(jax.ShapeDtypeStruct(tiles.shape, F32))
-        out_specs.append(block)
-    else:
-        out_shape += [jax.ShapeDtypeStruct((32, 128, 256), BF16), jax.ShapeDtypeStruct((16, 256, 128), BF16)]
-        out_specs += [vmem, vmem]
-        scratch = [pltpu.VMEM((32, 128, 256), F32), pltpu.VMEM((16, 256, 128), F32)]
     return pl.pallas_call(
-        functools.partial(tile_kernel, first, last),
-        grid=(slots // GROUP,),
+        kernel,
         out_shape=out_shape,
-        in_specs=[smem] * 4 + [block] + [vmem] * len(dense),
-        out_specs=out_specs,
+        in_specs=[smem] * 4 + [vmem] * len(dense),
+        out_specs=[pl.BlockSpec(memory_space=out_space)] * len(out_shape),
         scratch_shapes=scratch,
-        compiler_params=pltpu.CompilerParams(vmem_limit_bytes=LIMIT),
-    )(*scalars, tiles, *dense)
-
-
-def prep(counts, whiten):
+        compiler_params=pltpu.CompilerParams(vmem_limit_bytes=limit * MIB),
+    )(*scalars, *dense)
+
+
+def prep(counts, whiten, tiles):
+    mine = Place().mine
+    whiten = lax.dynamic_slice(whiten, (mine // 2, 0, mine % 2 * 256), (1, 512, 256)).reshape(512, 256)
     vmem = pl.BlockSpec(memory_space=pltpu.VMEM)
     n = 15 + 15 + 7
     shapes = ((16, 512, 128), (8, 512, 128), (16, 256, 256), (8, 256, 256))
     return pl.pallas_call(
         prep_kernel,
-        out_shape=[jax.ShapeDtypeStruct(s, BF16) for s in shapes],
-        in_specs=[vmem, pl.BlockSpec(memory_space=pl.ANY)],
-        out_specs=[vmem] * 4,
+        out_shape=[jax.ShapeDtypeStruct(s, BF16) for s in shapes] + [jax.ShapeDtypeStruct(tiles.shape, F32)],
+        in_specs=[pl.BlockSpec(memory_space=pltpu.HBM)] * 2 + [vmem],
+        out_specs=[vmem] * 5,
         scratch_shapes=[
+            pltpu.VMEM((16, 4096), jnp.int32),
             pltpu.VMEM((8, 16, 512), jnp.int16),
             pltpu.VMEM((16, 16, 512), jnp.int16),
-            pltpu.VMEM((512, 256), BF16),
-            pltpu.SemaphoreType.DMA,
+            pltpu.SemaphoreType.DMA((2,)),
             pltpu.SemaphoreType.DMA((2,)),
             pltpu.SemaphoreType.DMA((n,)),
             pltpu.SemaphoreType.DMA((n,)),
         ],
-        compiler_params=pltpu.CompilerParams(collective_id=0, has_side_effects=True, vmem_limit_bytes=LIMIT),
-    )(counts, whiten)
+        compiler_params=pltpu.CompilerParams(collective_id=0, has_side_effects=True, vmem_limit_bytes=PREP_MIB * MIB),
+    )(counts, tiles, whiten)
 
 
 def reduce_both(rp, cp, collective_id):
@@ -496,24 +534,33 @@
             pltpu.SemaphoreType.DMA((n,)),
         ],
         compiler_params=pltpu.CompilerParams(
-            collective_id=collective_id, has_side_effects=True, vmem_limit_bytes=LIMIT
+            collective_id=collective_id, has_side_effects=True, vmem_limit_bytes=12 * MIB
         ),
     )(rp.reshape(16, 256, 256), cp.reshape(8, 512, 128))
     return u.reshape(32, 128, 256), v.reshape(16, 256, 128)
 
 
 def local(counts, whiten, initial_tiles, tile_rows, tile_cols, tile_count):
-    tiles = initial_tiles.reshape(96, 128, 128)
     where_at = jnp.stack([lax.axis_index("row") * 32, lax.axis_index("col") * 16]).astype(jnp.int32)
     scalars = (tile_rows.reshape(96), tile_cols.reshape(96), tile_count.reshape(1), where_at)
-    xr, xc, xrt, xct = prep(counts, whiten)
+    xr, xc, xrt, xct, tiles = prep(counts, whiten, initial_tiles.reshape(96, 128, 128))
     xr, xc = xr.reshape(32, 256, 128), xc.reshape(16, 256, 128)
     xrt, xct = xrt.reshape(32, 128, 256), xct.reshape(16, 128, 256)
-    rp, cp = tile_call(True, False, scalars, tiles, (xr, xct))
+    omega_shape = jax.ShapeDtypeStruct(tiles.shape, F32)
+    part_shapes = [jax.ShapeDtypeStruct((32, 128, 256), BF16), jax.ShapeDtypeStruct((16, 256, 128), BF16)]
+    sums = [pltpu.VMEM((32, 128, 256), F32), pltpu.VMEM((16, 256, 128), F32)]
+    rp, cp = tile_call(first_kernel, scalars, (tiles, xr, xct), part_shapes, pltpu.VMEM, sums, 12)
     u, v = reduce_both(rp, cp, 1)
-    omega, rp, cp = tile_call(False, False, scalars, tiles, (u, v, xrt, xc, xr, xct))
+    omega, rp, cp = tile_call(
+        middle_kernel, scalars, (tiles, u, v, xrt, xc, xr, xct), [omega_shape] + part_shapes, pltpu.VMEM,
+        sums + [pltpu.VMEM((GROUP, 128, 128), BF16)], 12,
+    )
     u, v = reduce_both(rp, cp, 2)
-    omega, grad = tile_call(False, True, scalars, omega, (u, v, xrt, xc))
+    buffers = [pltpu.VMEM(tiles.shape, F32)] * 2 + [pltpu.VMEM((GROUP, 128, 128), F32)]
+    omega, grad = tile_call(
+        last_kernel, scalars, (omega, u, v, xrt, xc), [omega_shape] * 2, pltpu.HBM,
+        buffers + [pltpu.SemaphoreType.DMA((2, 96 // GROUP))], 20,
+    )
     return omega.reshape(initial_tiles.shape), grad.reshape(initial_tiles.shape)
 
 

time: 156 us -> 136 us (0.87)
  Pallas kernels: 145 us -> 132 us
  local copies, waits for them, and re-layouts: 8.7 us -> 1.92 us
    pallas_call x3, Pallas kernels: 27.9 us -> 18.6 us  [tile_call(): pl.pallas_call(kernel, out_shape=out_shape, in_specs=[smem] * 4 + [vmem]...]
    unnamed x12 -> x6, local copies, waits for them, and re-layouts: 8.7 us -> 0.95 us
    pallas_call x2, Pallas kernels: 81.8 us -> 78.7 us  [reduce_both(): pl.pallas_call(reduce_kernel, out_shape=[jax.ShapeDtypeStruct((16, 256, 2...]
where the time goes in v2:
time: 136 us
  Pallas kernels  132 us (97%)
  local copies, waits for them, and re-layouts  1.92 us (1%)
  between operations  1.44 us (1%)
    pallas_call x2, Pallas kernels, reduce_both(): pl.pallas_call(reduce_kernel, out_shape=[jax.ShapeDtypeStruct((16, 256, 2...  78.7 us
    pallas_call x1, Pallas kernels, prep(): pl.pallas_call(prep_kernel, out_shape=[jax.ShapeDtypeStruct(s, BF16) for...  34.8 us
    pallas_call x3, Pallas kernels, tile_call(): pl.pallas_call(kernel, out_shape=out_shape, in_specs=[smem] * 4 + [vmem]...  18.6 us

profile of v2, /device:TPU:1, one launch (start us, length us, event | category | flops | bytes accessed | tf_op | source)
XLA Modules:
  0.0 135.5 jit_solution(1945204027101982493)
XLA Ops:
  0.6 0.0 copy-start.2
  0.6 0.0 copy-start.1
  1.4 0.1 pad_add_fusion.where_at
  1.5 1.0 dynamic-slice_bitcast_fusion.whiten
  2.4 0.0 copy-start
  2.4 0.9 copy-done
  3.4 34.8 %shard_map.77 = (bf16[16,512,128]{2,1,0:T(8,128)(2,1)S(1)}, bf16[8,512,128]{2,1,0:T(8,128)(2,1)S(1)}, bf16[16,256,256]{2,1,0:T(8,128)(2,1)S(1)}, bf16[8,256,256]{2,1,0:T(8,128)(2,1)S(1)}, f32[96,128,128]{2,1,0:T(8,128)S(1)}) custom-call(s32[16,4096]{1,0:T(8,128)S(1)} %copy-done, f32[96,128,128]{2,1,0:T(8,128)} %bitcast.47, ...), custom_call_target="tpu_custom_call" | custom-call | tf_op jit(solution)/shard_map/pallas_call | solution.py:496
  38.2 0.0 copy-done.2
  38.2 0.0 copy-done.1
  38.2 4.4 %shard_map.78 = (bf16[32,128,256]{2,1,0:T(8,128)(2,1)S(1)}, bf16[16,256,128]{2,1,0:T(8,128)(2,1)S(1)}) custom-call(s32[96]{0:T(128)S(1)} %bitcast.41, s32[96]{0:T(128)S(1)} %bitcast.44, s32[1]{0:T(128)} %bitcast.22.count, s32[2]{0:T(128)S(1)} %pad_add_fusion.where_at, f32[96,128,128]{2,1,0:T(8,128)S(1)} %get-tuple-element.18.tiles, ...), custom_call_target="tpu_custom_call" | custom-call | tf_op jit(solution)/shard_map/pallas_call | solution.py:480
  42.6 39.3 %shard_map.79 = (bf16[16,256,256]{2,1,0:T(8,128)(2,1)S(1)}, bf16[8,512,128]{2,1,0:T(8,128)(2,1)S(1)}) custom-call(bf16[16,256,256]{2,1,0:T(8,128)(2,1)S(1)} %bitcast.35, bf16[8,512,128]{2,1,0:T(8,128)(2,1)S(1)} %bitcast.39), custom_call_target="tpu_custom_call" | custom-call | tf_op jit(solution)/shard_map/pallas_call | solution.py:517
  81.9 8.0 %shard_map.80 = (f32[96,128,128]{2,1,0:T(8,128)S(1)}, bf16[32,128,256]{2,1,0:T(8,128)(2,1)S(1)}, bf16[16,256,128]{2,1,0:T(8,128)(2,1)S(1)}) custom-call(s32[96]{0:T(128)S(1)} %bitcast.42, s32[96]{0:T(128)S(1)} %bitcast.45, s32[1]{0:T(128)} %bitcast.23.count, s32[2]{0:T(128)S(1)} %pad_add_fusion.where_at, f32[96,128,128]{2,1,0:T(8,128)S(1)} %get-tuple-element.18.tiles, ...), custom_call_target="tpu_custom_call" | custom-call | tf_op jit(solution)/shard_map/pallas_call | solution.py:480
  89.9 39.4 %shard_map.81 = (bf16[16,256,256]{2,1,0:T(8,128)(2,1)S(1)}, bf16[8,512,128]{2,1,0:T(8,128)(2,1)S(1)}) custom-call(bf16[16,256,256]{2,1,0:T(8,128)(2,1)S(1)} %bitcast.34, bf16[8,512,128]{2,1,0:T(8,128)(2,1)S(1)} %bitcast.38), custom_call_target="tpu_custom_call" | custom-call | tf_op jit(solution)/shard_map/pallas_call | solution.py:517
  129.2 6.3 %shard_map.82 = (f32[96,128,128]{2,1,0:T(8,128)}, f32[96,128,128]{2,1,0:T(8,128)}) custom-call(s32[96]{0:T(128)S(1)} %bitcast.43, s32[96]{0:T(128)S(1)} %bitcast.46, s32[1]{0:T(128)} %bitcast.24.count, s32[2]{0:T(128)S(1)} %pad_add_fusion.where_at, f32[96,128,128]{2,1,0:T(8,128)S(1)} %get-tuple-element.27.tiles, bf16[32,128,256]{2,1,0:T(8,128)(2,1)S(1)} %bitcast.36, ...), custom_call_target="tpu_custom_call" | custom-call | tf_op jit(solution)/shard_map/pallas_call | solution.py:480
Async XLA Ops:
  0.6 37.6 %copy-start.2 = (s32[1,1,96]{2,1,0:T(1,128)S(1)}, s32[1,1,96]{2,1,0:T(1,128)}, u32[]{:S(2)}) copy-start(s32[1,1,96]{2,1,0:T(1,128)} %param.10) | copy-start | bytes 1156
  0.6 37.6 %copy-start.1 = (s32[1,1,96]{2,1,0:T(1,128)S(1)}, s32[1,1,96]{2,1,0:T(1,128)}, u32[]{:S(2)}) copy-start(s32[1,1,96]{2,1,0:T(1,128)} %param.9) | copy-start | bytes 1156
  2.4 1.0 copy-start

commit v3 on v2

v3 whole, which is shorter than its diff:
```python
import functools

import jax
import jax.numpy as jnp
from jax import lax
from jax.experimental import pallas as pl
from jax.experimental.pallas import tpu as pltpu
from jax.sharding import PartitionSpec as P

step_size = 0.08
penalty = 1.0
epsilon = 1e-05
MESH = pl.DeviceIdType.MESH
F32 = jnp.float32
BF16 = jnp.bfloat16
GROUP = 8
MIB = 2**20
PREP_MIB = 39


class Place:
    def __init__(self):
        self.row = lax.axis_index("row")
        self.col = lax.axis_index("col")
        self.y, self.zh = self.row // 2, self.row % 2
        self.zl, self.x, self.core = self.col // 8, (self.col // 2) % 4, self.col % 2
        self.mine = self.core * 8 + self.x * 2 + self.zl
        self.mine_col = self.row

    def at(self, row=None, col=None):
        return (self.row if row is None else row, self.col if col is None else col)

    def xpeer(self, d):
        return self.at(col=self.zl * 8 + ((self.x + d) % 4) * 2 + self.core)

    def ypeer(self, d):
        return self.at(row=((self.y + d) % 4) * 2 + self.zh)

    def zlpeer(self):
        return self.at(col=(1 - self.zl) * 8 + self.x * 2 + self.core)

    def zhpeer(self):
        return self.at(row=self.y * 2 + 1 - self.zh)

    def sibling(self):
        return self.at(col=self.zl * 8 + self.x * 2 + 1 - self.core)


class Wire:
    def __init__(self, send_sem, recv_sem):
        self.send_sem, self.recv_sem = send_sem, recv_sem
        self.copies = {}

    def send(self, name, src, dst, device):
        i = len(self.copies)
        copy = pltpu.make_async_remote_copy(
            src_ref=src, dst_ref=dst, send_sem=self.send_sem.at[i],
            recv_sem=self.recv_sem.at[i], device_id=device, device_id_type=MESH,
        )
        copy.start()
        self.copies[name] = copy

    def recv(self, *names):
        for name in names:
            self.copies[name].wait_recv()

    def drain(self):
        for copy in self.copies.values():
            copy.wait_send()


class Stream:
    def __init__(self, part, parts):
        self.part, self.parts = part, parts

    def rows(self, ref):
        size = ref.shape[-2] // self.parts
        return pl.ds(self.part * size, size)

    def cut(self, ref, i):
        return ref.at[i, self.rows(ref)]


class Gather:
    def __init__(self, wire, stream, tag, out, base, position, z, ring, sibling, done, relayed):
        self.w, self.stream, self.tag, self.out = wire, stream, f"{tag}{stream.part}", out
        self.base, self.position, self.z = base, position, z
        self.ring, self.sibling, self.done, self.relayed = ring, sibling, done, relayed
        self.shared = []

    def slot(self, d, other):
        z = 1 - self.z if other else self.z
        return self.base + ((self.position + d) % 4) * 2 + z

    def pass_on(self, name, slot, device):
        part = self.stream.cut(self.out, slot)
        self.w.send(f"{self.tag}{name}", part, part, device)

    def have(self, d, other):
        s = self.slot(d, other)
        if self.sibling is not None:
            self.pass_on(f"core{d}{other}", s, self.sibling)
            self.shared.append((d, other))
        self.done(s)

    def exchange(self, zpeer):
        self.pass_on("z", self.slot(0, 0), zpeer)

    def exchanged(self):
        self.w.recv(self.tag + "z")

    def start(self, other):
        for d in (1, 3) if self.relayed else (1, 3, 2):
            self.pass_on(f"{other}{d}", self.slot(0, other), self.ring(d))
        self.have(0, other)

    def arrive(self, other, d):
        self.w.recv(f"{self.tag}{other}{d}")
        if self.relayed and (other, d) in ((0, 1), (1, 3)):
            self.pass_on(f"{other}2", self.slot(4 - d, other), self.ring(d))
        self.have(4 - d, other)

    def rest(self):
        for d, other in self.shared:
            self.w.recv(f"{self.tag}core{d}{other}")
            self.done(self.slot(d, other) + 8 - 2 * self.base)


def arrivals(gathers):
    for other in (0, 1):
        for d in (1, 3, 2):
            for gather in gathers:
                gather.arrive(other, d)
    for gather in gathers:
        gather.rest()


def row_gather(wire, stream, place, out, done, relayed):
    return Gather(
        wire, stream, "r", out, place.core * 8, place.x, place.zl, place.xpeer, place.sibling(), done, relayed
    )


def col_gather(wire, stream, place, out, done, relayed):
    return Gather(wire, stream, "c", out, 0, place.y, place.zh, place.ypeer, None, done, relayed)


PARTS = 2


def greet(devices):
    barrier = pltpu.get_barrier_semaphore()
    for device in devices:
        pl.semaphore_signal(barrier, inc=1, device_id=device, device_id_type=MESH)
    return barrier


def prep_kernel(
    counts_hbm, tiles_hbm, whiten, xr, xc, xrt, xct, tiles, counts, packed, landed, wsem, lsem, send_sem, recv_sem
):
    place = Place()
    block = place.mine // 2
    to_row, to_col = place.x * 2 + place.zl, 2 * place.row + place.core
    from_row, from_col = place.col // 2, (place.row % 2) * 8 + (place.row // 2) * 2 + place.core
    moves = jnp.logical_or(to_row != place.row, to_col != place.col)
    peers = [place.at(col=(place.col + d) % 16) for d in range(1, 16)]
    peers += [place.ypeer(d) for d in (1, 2, 3)] + [place.zhpeer()]
    barrier = greet(peers)

    @pl.when(moves)
    def _():
        for device in ((to_row, to_col), (from_row, from_col)):
            pl.semaphore_signal(barrier, inc=1, device_id=device, device_id_type=MESH)

    counted = pltpu.make_async_copy(counts_hbm, counts, wsem.at[0])
    tiled = pltpu.make_async_copy(tiles_hbm, tiles, wsem.at[1])
    counted.start()
    tiled.start()
    counted.wait()
    for b in range(8):
        packed[b] = counts[:, b * 512 : (b + 1) * 512].astype(jnp.int16)
    pl.semaphore_wait(barrier, len(peers) + 2 * moves.astype(jnp.int32))

    wire = Wire(send_sem, recv_sem)
    for d in range(1, 16):
        c = (place.col + d) % 16
        b = (c % 2) * 4 + (c // 2) % 4
        wire.send(f"a{d}", packed.at[b], landed.at[place.col], place.at(col=c))
    landed[place.col] = packed[block]
    wire.recv(*[f"a{d}" for d in range(1, 16)])
    logged = jnp.log(1.0 + landed[...].astype(jnp.int32).astype(F32)).reshape(256, 512)
    mean = jnp.mean(logged, axis=0, keepdims=True)
    centered = logged - mean
    variance = jnp.mean(centered * centered, axis=0, keepdims=True)
    standard = (centered * lax.rsqrt(variance + epsilon)).astype(BF16)
    whitened = jnp.dot(standard, whiten[...], preferred_element_type=F32).astype(BF16)
    pair = block * 2
    for j in range(4):
        xr[pair + j // 2, j % 2 * 256 : (j % 2 + 1) * 256] = whitened[:, j * 128 : (j + 1) * 128]

    def turn(source, target, part):
        def done(s):
            for t in range(2 // PARTS * part, 2 // PARTS * (part + 1)):
                target[s, t * 128 : (t + 1) * 128] = source[s, t * 256 : (t + 1) * 256].T

        return done

    streams = [Stream(p, PARTS) for p in range(PARTS)]
    rows = [row_gather(wire, t, place, xr, turn(xr, xrt, t.part), True) for t in streams]
    cols = [col_gather(wire, t, place, xc, turn(xc, xct, t.part), True) for t in streams]
    hop = pltpu.make_async_remote_copy(
        src_ref=xr.at[place.mine], dst_ref=xc.at[to_row], send_sem=lsem.at[0],
        recv_sem=lsem.at[1], device_id=(to_row, to_col), device_id_type=MESH,
    )

    @pl.when(moves)
    def _():
        hop.start()

    @pl.when(jnp.logical_not(moves))
    def _():
        xc[place.mine_col] = xr[place.mine]

    for row in rows:
        row.start(0)
        row.start(1)

    @pl.when(moves)
    def _():
        hop.wait_recv()

    for col in cols:
        col.exchange(place.zhpeer())
        col.start(0)
    for row in rows:
        row.arrive(0, 1)
        row.arrive(1, 3)
    for col in cols:
        col.arrive(0, 1)
        col.exchanged()
        col.start(1)
    for col in cols:
        col.arrive(0, 3)
    for other, d in ((0, 3), (1, 1), (0, 2), (1, 2)):
        for row in rows:
            row.arrive(other, d)
    for other, d in ((1, 3), (1, 1), (0, 2), (1, 2)):
        for col in cols:
            col.arrive(other, d)
    for row in rows:
        row.rest()
    tiled.wait()
    wire.drain()

    @pl.when(moves)
    def _():
        hop.wait_send()


def add(*parts):
    total = parts[0].astype(F32)
    for part in parts[1:]:
        total = total + part.astype(F32)
    return total


class Scatter:
    def __init__(self, wire, stream, tag, terms, slot, land, ztemp, keep, z, ring, zpeer):
        self.w, self.stream, self.tag = wire, stream, f"{tag}{stream.part}"
        self.terms, self.slot, self.land, self.ztemp, self.keep = terms, slot, land, ztemp, keep
        self.z, self.ring, self.zpeer = z, ring, zpeer

    def term(self, d, e):
        return self.stream.cut(self.terms, self.slot(d, e))

    def landed(self, i):
        return self.stream.cut(self.land, i)

    def put(self, name, i, src, device):
        self.w.send(self.tag + name, src, self.landed(i), device)

    def first(self):
        self.put("A1", 0, self.term(2, 0), self.ring(1))
        self.put("B1", 1, self.term(2, 1), self.ring(3))

    def second(self):
        self.put("A2", 2, self.term(1, 1), self.ring(1))
        self.put("B2", 3, self.term(3, 0), self.ring(3))

    def merge(self):
        for name, i, d, e, then in (("A1", 0, 1, 0, "A3"), ("B1", 1, 3, 1, "B3")):
            self.w.recv(self.tag + name)
            here = self.landed(i)
            here[...] = add(self.term(d, e)[...], here[...]).astype(BF16)
            self.put(then, 4 + i, here, self.ring(d))

    def cross(self):
        self.w.recv(*[self.tag + n for n in ("B2", "A2", "A3", "B3")])
        own = [
            add(self.term(0, e)[...], self.landed(i)[...], self.landed(j)[...]) for e, i, j in ((0, 3, 4), (1, 2, 5))
        ]
        mine = self.z == 0
        out = self.stream.cut(self.ztemp, 0)
        out[...] = jnp.where(mine, own[1], own[0]).astype(BF16)
        self.w.send(self.tag + "Z", out, self.stream.cut(self.ztemp, 1), self.zpeer)
        self.keep[self.stream.rows(self.keep)] = jnp.where(mine, own[0], own[1])

    def last(self, out, slot):
        self.w.recv(self.tag + "Z")
        got = self.stream.cut(self.ztemp, 1)[...]
        self.stream.cut(out, slot)[...] = add(self.keep[self.stream.rows(self.keep)], got).astype(BF16)


def reduce_kernel(rfull, cfull, u, v, rp, cp, pair, summed, rland, rtemp, rkeep, cland, ctemp, ckeep, send_sem, recv_sem):
    place = Place()
    peers = [place.sibling(), place.zlpeer(), place.zhpeer()]
    peers += [place.xpeer(d) for d in (1, 2, 3)] + [place.ypeer(d) for d in (1, 2, 3)]
    barrier = greet(peers)
    rp[...] = rfull[...].astype(BF16)
    cp[...] = cfull[...].astype(BF16)
    pl.semaphore_wait(barrier, len(peers))
    wire = Wire(send_sem, recv_sem)
    here, there = place.core * 8, 8 - place.core * 8

    def rslot(d, e):
        return ((place.x + d) % 4) * 2 + e

    def cslot(d, e):
        return ((place.y + d) % 4) * 2 + e

    streams = [Stream(p, PARTS) for p in range(PARTS)]
    cols = [
        Scatter(wire, t, "cs", cp, cslot, cland, ctemp, ckeep, place.zh, place.ypeer, place.zhpeer()) for t in streams
    ]
    rows = [
        Scatter(wire, t, "rs", summed, rslot, rland, rtemp, rkeep, place.zl, place.xpeer, place.zlpeer())
        for t in streams
    ]
    order = ((2, 0), (2, 1), (1, 1), (3, 0), (1, 0), (3, 1), (0, 0), (0, 1))
    for t in streams:
        for d, e in order:
            s = rslot(d, e)
            wire.send(f"s{t.part}{d}{e}", t.cut(rp, there + s), t.cut(pair, s), place.sibling())
    for col in cols:
        col.first()
        col.second()

    def join(t, which):
        for d, e in which:
            s = rslot(d, e)
            wire.recv(f"s{t.part}{d}{e}")
            t.cut(summed, s)[...] = add(t.cut(rp, here + s)[...], t.cut(pair, s)[...]).astype(BF16)

    for t, row in zip(streams, rows):
        join(t, order[:2])
        row.first()
        join(t, order[2:4])
        row.second()
    for t, row, col in zip(streams, rows, cols):
        col.merge()
        join(t, order[4:6])
        row.merge()
    for t in streams:
        join(t, order[6:])
    for row, col in zip(rows, cols):
        col.cross()
        row.cross()
    nothing = lambda s: None
    rgs = [row_gather(wire, t, place, u, nothing, False) for t in streams]
    cgs = [col_gather(wire, t, place, v, nothing, False) for t in streams]
    for row, col, rg, cg in zip(rows, cols, rgs, cgs):
        col.last(v, place.mine_col)
        cg.exchange(place.zhpeer())
        cg.start(0)
        row.last(u, place.mine)
        rg.exchange(place.zlpeer())
        rg.start(0)
    for rg, cg in zip(rgs, cgs):
        cg.exchanged()
        cg.start(1)
        rg.exchanged()
        rg.start(1)
    arrivals(cgs + rgs)
    wire.drain()


def live_groups(count):
    return (count[0] + GROUP - 1) // GROUP


def gradient(k, live, rows, cols, u, v, xrt, xc):
    sr, sc = rows[k], cols[k]
    left = jnp.dot(u[sr], xc[sc], preferred_element_type=F32)
    right = jnp.dot(xrt[sr], v[sc], preferred_element_type=F32)
    return jnp.where(k < live, (left + right) * (0.5 / 256), 0.0)


def shrunk(moved):
    t = step_size * penalty
    return moved - jnp.clip(moved, -t, t)


def fix_diagonal(g, live, rows, cols, where_at, grads, base, tiles, omega_out):
    for j in range(GROUP):
        k = g * GROUP + j

        @pl.when(jnp.logical_and(k < live, where_at[0] + rows[k] == where_at[1] + cols[k]))
        def _():
            moved = tiles[k] - step_size * grads[base + j]
            diagonal = 0.5 * (moved + jnp.sqrt(moved * moved + 4.0 * step_size))
            row = lax.broadcasted_iota(jnp.int32, (128, 128), 0)
            col = lax.broadcasted_iota(jnp.int32, (128, 128), 1)
            omega_out[k] = jnp.where(row == col, diagonal, omega_out[k])


def products(k, low, rows, cols, xr, xct, rp, cp):
    sr, sc = rows[k], cols[k]
    rp[sr] += jnp.dot(low, xct[sc], preferred_element_type=F32)
    cp[sc] += jnp.dot(xr[sr], low, preferred_element_type=F32)


def first_kernel(rows, cols, count, where_at, tiles, xr, xct, rp, cp):
    rp[...] = jnp.zeros_like(rp)
    cp[...] = jnp.zeros_like(cp)
    live = count[0]

    def group(g, _):
        for j in range(GROUP):
            k = g * GROUP + j
            low = jnp.where(k < live, tiles[k], 0.0).astype(BF16)
            products(k, low, rows, cols, xr, xct, rp, cp)
        return 0

    lax.fori_loop(0, live_groups(count), group, 0)


def middle_kernel(rows, cols, count, where_at, tiles, u, v, xrt, xc, xr, xct, omega_out, rp, cp, grads):
    rp[...] = jnp.zeros_like(rp)
    cp[...] = jnp.zeros_like(cp)
    live = count[0]

    def group(g, _):
        for j in range(GROUP):
            k = g * GROUP + j
            grad = gradient(k, live, rows, cols, u, v, xrt, xc)
            grads[j] = grad
            omega_out[k] = shrunk(jnp.where(k < live, tiles[k], 0.0) - step_size * grad)
        fix_diagonal(g, live, rows, cols, where_at, grads, 0, tiles, omega_out)
        for j in range(GROUP):
            k = g * GROUP + j
            products(k, omega_out[k].astype(BF16), rows, cols, xr, xct, rp, cp)
        return 0

    lax.fori_loop(0, live_groups(count), group, 0)


def last_kernel(rows, cols, count, where_at, tiles, u, v, xrt, xc, omega_out, grad_out, obuf, gbuf, zeros, sem):
    live = count[0]
    groups, total = live_groups(count), omega_out.shape[0] // GROUP

    def writes(g, o, d):
        here = pl.ds(g * GROUP, GROUP)
        return (
            pltpu.make_async_copy(o, omega_out.at[here], sem.at[0, g]),
            pltpu.make_async_copy(d, grad_out.at[here], sem.at[1, g]),
        )

    zeros[...] = jnp.zeros_like(zeros)

    def dead(g, _):
        for copy in writes(g, zeros, zeros):
            copy.start()
        return 0

    lax.fori_loop(groups, total, dead, 0)

    def group(g, _):
        for j in range(GROUP):
            k = g * GROUP + j
            grad = gradient(k, live, rows, cols, u, v, xrt, xc)
            gbuf[k] = grad
            obuf[k] = shrunk(jnp.where(k < live, tiles[k], 0.0) - step_size * grad)
        fix_diagonal(g, live, rows, cols, where_at, gbuf, g * GROUP, tiles, obuf)
        here = pl.ds(g * GROUP, GROUP)
        for copy in writes(g, obuf.at[here], gbuf.at[here]):
            copy.start()
        return 0

    lax.fori_loop(0, groups, group, 0)

    def wait(g, _):
        for copy in writes(g, zeros, zeros):
            copy.wait()
        return 0

    lax.fori_loop(0, total, wait, 0)


def tile_call(kernel, scalars, dense, out_shape, out_space, scratch, limit):
    smem = pl.BlockSpec(memory_space=pltpu.SMEM)
    vmem = pl.BlockSpec(memory_space=pltpu.VMEM)
    return pl.pallas_call(
        kernel,
        out_shape=out_shape,
        in_specs=[smem] * 4 + [vmem] * len(dense),
        out_specs=[pl.BlockSpec(memory_space=out_space)] * len(out_shape),
        scratch_shapes=scratch,
        compiler_params=pltpu.CompilerParams(vmem_limit_bytes=limit * MIB),
    )(*scalars, *dense)


def prep(counts, whiten, tiles):
    whiten = lax.dynamic_slice(whiten, (Place().mine // 2, 0, 0), (1, 512, 512)).reshape(512, 512)
    vmem = pl.BlockSpec(memory_space=pltpu.VMEM)
    n = 15 + PARTS * (14 + 7)
    shapes = ((16, 512, 128), (8, 512, 128), (16, 256, 256), (8, 256, 256))
    return pl.pallas_call(
        prep_kernel,
        out_shape=[jax.ShapeDtypeStruct(s, BF16) for s in shapes] + [jax.ShapeDtypeStruct(tiles.shape, F32)],
        in_specs=[pl.BlockSpec(memory_space=pltpu.HBM)] * 2 + [vmem],
        out_specs=[vmem] * 5,
        scratch_shapes=[
            pltpu.VMEM((16, 4096), jnp.int32),
            pltpu.VMEM((8, 16, 512), jnp.int16),
            pltpu.VMEM((16, 16, 512), jnp.int16),
            pltpu.SemaphoreType.DMA((2,)),
            pltpu.SemaphoreType.DMA((2,)),
            pltpu.SemaphoreType.DMA((n,)),
            pltpu.SemaphoreType.DMA((n,)),
        ],
        compiler_params=pltpu.CompilerParams(collective_id=0, has_side_effects=True, vmem_limit_bytes=PREP_MIB * MIB),
    )(counts, tiles, whiten)


def reduce_both(rp, cp, collective_id):
    vmem = pl.BlockSpec(memory_space=pltpu.VMEM)
    n = PARTS * (8 + 7 + 7 + 15 + 7)
    u, v = pl.pallas_call(
        reduce_kernel,
        out_shape=[jax.ShapeDtypeStruct((16, 256, 256), BF16), jax.ShapeDtypeStruct((8, 512, 128), BF16)],
        in_specs=[vmem] * 2,
        out_specs=[vmem] * 2,
        scratch_shapes=[
            pltpu.VMEM((16, 256, 256), BF16),
            pltpu.VMEM((8, 512, 128), BF16),
            pltpu.VMEM((8, 256, 256), BF16),
            pltpu.VMEM((8, 256, 256), BF16),
            pltpu.VMEM((6, 256, 256), BF16),
            pltpu.VMEM((2, 256, 256), BF16),
            pltpu.VMEM((256, 256), F32),
            pltpu.VMEM((6, 512, 128), BF16),
            pltpu.VMEM((2, 512, 128), BF16),
            pltpu.VMEM((512, 128), F32),
            pltpu.SemaphoreType.DMA((n,)),
            pltpu.SemaphoreType.DMA((n,)),
        ],
        compiler_params=pltpu.CompilerParams(
            collective_id=collective_id, has_side_effects=True, vmem_limit_bytes=12 * MIB
        ),
    )(rp.reshape(16, 256, 256), cp.reshape(8, 512, 128))
    return u.reshape(32, 128, 256), v.reshape(16, 256, 128)


def local(counts, whiten, initial_tiles, tile_rows, tile_cols, tile_count):
    where_at = jnp.stack([lax.axis_index("row") * 32, lax.axis_index("col") * 16]).astype(jnp.int32)
    scalars = (tile_rows.reshape(96), tile_cols.reshape(96), tile_count.reshape(1), where_at)
    xr, xc, xrt, xct, tiles = prep(counts, whiten, initial_tiles.reshape(96, 128, 128))
    xr, xc = xr.reshape(32, 256, 128), xc.reshape(16, 256, 128)
    xrt, xct = xrt.reshape(32, 128, 256), xct.reshape(16, 128, 256)
    omega_shape = jax.ShapeDtypeStruct(tiles.shape, F32)
    part_shapes = [jax.ShapeDtypeStruct((32, 128, 256), F32), jax.ShapeDtypeStruct((16, 256, 128), F32)]
    rp, cp = tile_call(first_kernel, scalars, (tiles, xr, xct), part_shapes, pltpu.VMEM, [], 10)
    u, v = reduce_both(rp, cp, 1)
    omega, rp, cp = tile_call(
        middle_kernel, scalars, (tiles, u, v, xrt, xc, xr, xct), [omega_shape] + part_shapes, pltpu.VMEM,
        [pltpu.VMEM((GROUP, 128, 128), F32)], 10,
    )
    u, v = reduce_both(rp, cp, 2)
    buffers = [pltpu.VMEM(tiles.shape, F32)] * 2 + [pltpu.VMEM((GROUP, 128, 128), F32)]
    omega, grad = tile_call(
        last_kernel, scalars, (omega, u, v, xrt, xc), [omega_shape] * 2, pltpu.HBM,
        buffers + [pltpu.SemaphoreType.DMA((2, 96 // GROUP))], 20,
    )
    return omega.reshape(initial_tiles.shape), grad.reshape(initial_tiles.shape)


def solution(mesh):
    in_specs = (
        P("col", "row"),
        P("row", None, None),
        P("row", "col", None, None, None),
        P("row", "col", None),
        P("row", "col", None),
        P("row", "col"),
    )
    out_specs = (P("row", "col", None, None, None), P("row", "col", None, None, None))
    return jax.shard_map(local, mesh=mesh, in_specs=in_specs, out_specs=out_specs, check_vma=False)
```

time: 136 us -> 129 us (0.949)
  Pallas kernels: 132 us -> 125 us
    pallas_call x2, Pallas kernels: 78.7 us -> 70.2 us  [reduce_both(): pl.pallas_call(reduce_kernel, out_shape=[jax.ShapeDtypeStruct((16, 256, 2...]
    pallas_call x3, Pallas kernels: 18.6 us -> 20.4 us  [tile_call(): pl.pallas_call(kernel, out_shape=out_shape, in_specs=[smem] * 4 + [vmem]...]
where the time goes in v3:
time: 129 us
  Pallas kernels  125 us (97%)
  local copies, waits for them, and re-layouts  2.03 us (2%)
  between operations  1.43 us (1%)
    pallas_call x2, Pallas kernels, reduce_both(): pl.pallas_call(reduce_kernel, out_shape=[jax.ShapeDtypeStruct((16, 256, 2...  70.2 us
    pallas_call x1, Pallas kernels, prep(): pl.pallas_call(prep_kernel, out_shape=[jax.ShapeDtypeStruct(s, BF16) for...  34.5 us
    pallas_call x3, Pallas kernels, tile_call(): pl.pallas_call(kernel, out_shape=out_shape, in_specs=[smem] * 4 + [vmem]...  20.4 us

profile of v3, /device:TPU:1, one launch (start us, length us, event | category | flops | bytes accessed | tf_op | source)
XLA Modules:
  0.0 128.7 jit_solution(15977452910123200337)
XLA Ops:
  0.6 0.0 copy-start.2
  0.6 0.0 copy-start.1
  1.4 0.1 pad_add_fusion.where_at
  1.4 1.1 dynamic-slice_bitcast_fusion.whiten
  2.5 0.0 copy-start
  2.5 0.9 copy-done
  3.5 34.5 %shard_map.77 = (bf16[16,512,128]{2,1,0:T(8,128)(2,1)S(1)}, bf16[8,512,128]{2,1,0:T(8,128)(2,1)S(1)}, bf16[16,256,256]{2,1,0:T(8,128)(2,1)S(1)}, bf16[8,256,256]{2,1,0:T(8,128)(2,1)S(1)}, f32[96,128,128]{2,1,0:T(8,128)S(1)}) custom-call(s32[16,4096]{1,0:T(8,128)S(1)} %copy-done, f32[96,128,128]{2,1,0:T(8,128)} %bitcast.47, ...), custom_call_target="tpu_custom_call" | custom-call | tf_op jit(solution)/shard_map/pallas_call | solution.py:517
  37.9 0.0 copy-done.2
  38.0 0.0 copy-done.1
  38.0 4.5 %shard_map.78 = (f32[32,128,256]{2,1,0:T(8,128)S(1)}, f32[16,256,128]{2,1,0:T(8,128)S(1)}) custom-call(s32[96]{0:T(128)S(1)} %bitcast.41, s32[96]{0:T(128)S(1)} %bitcast.44, s32[1]{0:T(128)} %bitcast.22.count, s32[2]{0:T(128)S(1)} %pad_add_fusion.where_at, f32[96,128,128]{2,1,0:T(8,128)S(1)} %get-tuple-element.18.tiles, bf16[32,256,128]{2,1,0:T(8,128)(2,1)S(1)} %bitcast.25, ...), custom_call_target="tpu_custom_call" | custom-call | tf_op jit(solution)/shard_map/pallas_call | solution.py:502
  42.5 35.6 %shard_map.79 = (bf16[16,256,256]{2,1,0:T(8,128)(2,1)S(1)}, bf16[8,512,128]{2,1,0:T(8,128)(2,1)S(1)}) custom-call(f32[16,256,256]{2,1,0:T(8,128)S(1)} %bitcast.32, f32[8,512,128]{2,1,0:T(8,128)S(1)} %bitcast.37), custom_call_target="tpu_custom_call" | custom-call | tf_op jit(solution)/shard_map/pallas_call | solution.py:538
  78.1 9.3 %shard_map.80 = (f32[96,128,128]{2,1,0:T(8,128)S(1)}, f32[32,128,256]{2,1,0:T(8,128)S(1)}, f32[16,256,128]{2,1,0:T(8,128)S(1)}) custom-call(s32[96]{0:T(128)S(1)} %bitcast.42, s32[96]{0:T(128)S(1)} %bitcast.45, s32[1]{0:T(128)} %bitcast.23.count, s32[2]{0:T(128)S(1)} %pad_add_fusion.where_at, f32[96,128,128]{2,1,0:T(8,128)S(1)} %get-tuple-element.18.tiles, ...), custom_call_target="tpu_custom_call" | custom-call | tf_op jit(solution)/shard_map/pallas_call | solution.py:502
  87.4 34.6 %shard_map.81 = (bf16[16,256,256]{2,1,0:T(8,128)(2,1)S(1)}, bf16[8,512,128]{2,1,0:T(8,128)(2,1)S(1)}) custom-call(f32[16,256,256]{2,1,0:T(8,128)S(1)} %bitcast.31, f32[8,512,128]{2,1,0:T(8,128)S(1)} %bitcast.36), custom_call_target="tpu_custom_call" | custom-call | tf_op jit(solution)/shard_map/pallas_call | solution.py:538
  122.0 6.7 %shard_map.82 = (f32[96,128,128]{2,1,0:T(8,128)}, f32[96,128,128]{2,1,0:T(8,128)}) custom-call(s32[96]{0:T(128)S(1)} %bitcast.43, s32[96]{0:T(128)S(1)} %bitcast.46, s32[1]{0:T(128)} %bitcast.24.count, s32[2]{0:T(128)S(1)} %pad_add_fusion.where_at, f32[96,128,128]{2,1,0:T(8,128)S(1)} %get-tuple-element.27.tiles, bf16[32,128,256]{2,1,0:T(8,128)(2,1)S(1)} %bitcast.38, ...), custom_call_target="tpu_custom_call" | custom-call | tf_op jit(solution)/shard_map/pallas_call | solution.py:502
Async XLA Ops:
  0.6 37.3 %copy-start.2 = (s32[1,1,96]{2,1,0:T(1,128)S(1)}, s32[1,1,96]{2,1,0:T(1,128)}, u32[]{:S(2)}) copy-start(s32[1,1,96]{2,1,0:T(1,128)} %param.10) | copy-start | bytes 1156
  0.6 37.3 %copy-start.1 = (s32[1,1,96]{2,1,0:T(1,128)S(1)}, s32[1,1,96]{2,1,0:T(1,128)}, u32[]{:S(2)}) copy-start(s32[1,1,96]{2,1,0:T(1,128)} %param.9) | copy-start | bytes 1156
  2.5 1.0 copy-start

commit v4 on v3

--- a/solution.py
+++ b/solution.py
@@ -13,9 +13,9 @@
 MESH = pl.DeviceIdType.MESH
 F32 = jnp.float32
 BF16 = jnp.bfloat16
-GROUP = 8
+GROUP = 24
 MIB = 2**20
-PREP_MIB = 39
+PREP_MIB = 41
 
 
 class Place:
@@ -156,7 +156,7 @@
 
 
 def prep_kernel(
-    counts_hbm, tiles_hbm, whiten, xr, xc, xrt, xct, tiles, counts, packed, landed, wsem, lsem, send_sem, recv_sem
+    counts_hbm, tiles_hbm, whiten, xc, xrt, xct, tiles, xr, counts, packed, landed, wsem, lsem, send_sem, recv_sem
 ):
     place = Place()
     block = place.mine // 2
@@ -305,10 +305,11 @@
         self.w.send(self.tag + "Z", out, self.stream.cut(self.ztemp, 1), self.zpeer)
         self.keep[self.stream.rows(self.keep)] = jnp.where(mine, own[0], own[1])
 
-    def last(self, out, slot):
+    def last(self, out, slot, turned):
         self.w.recv(self.tag + "Z")
         got = self.stream.cut(self.ztemp, 1)[...]
-        self.stream.cut(out, slot)[...] = add(self.keep[self.stream.rows(self.keep)], got).astype(BF16)
+        total = add(self.keep[self.stream.rows(self.keep)], got).astype(BF16)
+        self.stream.cut(out, slot)[...] = total.T if turned else total
 
 
 def reduce_kernel(rfull, cfull, u, v, rp, cp, pair, summed, rland, rtemp, rkeep, cland, ctemp, ckeep, send_sem, recv_sem):
@@ -369,10 +370,10 @@
     rgs = [row_gather(wire, t, place, u, nothing, False) for t in streams]
     cgs = [col_gather(wire, t, place, v, nothing, False) for t in streams]
     for row, col, rg, cg in zip(rows, cols, rgs, cgs):
-        col.last(v, place.mine_col)
+        col.last(v, place.mine_col, True)
         cg.exchange(place.zhpeer())
         cg.start(0)
-        row.last(u, place.mine)
+        row.last(u, place.mine, False)
         rg.exchange(place.zlpeer())
         rg.start(0)
     for rg, cg in zip(rgs, cgs):
@@ -413,13 +414,13 @@
             omega_out[k] = jnp.where(row == col, diagonal, omega_out[k])
 
 
-def products(k, low, rows, cols, xr, xct, rp, cp):
+def products(k, low, rows, cols, xrt, xct, rp, cp):
     sr, sc = rows[k], cols[k]
     rp[sr] += jnp.dot(low, xct[sc], preferred_element_type=F32)
-    cp[sc] += jnp.dot(xr[sr], low, preferred_element_type=F32)
-
-
-def first_kernel(rows, cols, count, where_at, tiles, xr, xct, rp, cp):
+    cp[sc] += jnp.dot(low.T, xrt[sr], preferred_element_type=F32)
+
+
+def first_kernel(rows, cols, count, where_at, tiles, xrt, xct, rp, cp):
     rp[...] = jnp.zeros_like(rp)
     cp[...] = jnp.zeros_like(cp)
     live = count[0]
@@ -428,13 +429,13 @@
         for j in range(GROUP):
             k = g * GROUP + j
             low = jnp.where(k < live, tiles[k], 0.0).astype(BF16)
-            products(k, low, rows, cols, xr, xct, rp, cp)
+            products(k, low, rows, cols, xrt, xct, rp, cp)
         return 0
 
     lax.fori_loop(0, live_groups(count), group, 0)
 
 
-def middle_kernel(rows, cols, count, where_at, tiles, u, v, xrt, xc, xr, xct, omega_out, rp, cp, grads):
+def middle_kernel(rows, cols, count, where_at, tiles, u, v, xrt, xc, xct, omega_out, rp, cp, grads):
     rp[...] = jnp.zeros_like(rp)
     cp[...] = jnp.zeros_like(cp)
     live = count[0]
@@ -448,7 +449,7 @@
         fix_diagonal(g, live, rows, cols, where_at, grads, 0, tiles, omega_out)
         for j in range(GROUP):
             k = g * GROUP + j
-            products(k, omega_out[k].astype(BF16), rows, cols, xr, xct, rp, cp)
+            products(k, omega_out[k].astype(BF16), rows, cols, xrt, xct, rp, cp)
         return 0
 
     lax.fori_loop(0, live_groups(count), group, 0)
@@ -513,13 +514,14 @@
     whiten = lax.dynamic_slice(whiten, (Place().mine // 2, 0, 0), (1, 512, 512)).reshape(512, 512)
     vmem = pl.BlockSpec(memory_space=pltpu.VMEM)
     n = 15 + PARTS * (14 + 7)
-    shapes = ((16, 512, 128), (8, 512, 128), (16, 256, 256), (8, 256, 256))
+    shapes = ((8, 512, 128), (16, 256, 256), (8, 256, 256))
     return pl.pallas_call(
         prep_kernel,
         out_shape=[jax.ShapeDtypeStruct(s, BF16) for s in shapes] + [jax.ShapeDtypeStruct(tiles.shape, F32)],
         in_specs=[pl.BlockSpec(memory_space=pltpu.HBM)] * 2 + [vmem],
-        out_specs=[vmem] * 5,
+        out_specs=[vmem] * 4,
         scratch_shapes=[
+            pltpu.VMEM((16, 512, 128), BF16),
             pltpu.VMEM((16, 4096), jnp.int32),
             pltpu.VMEM((8, 16, 512), jnp.int16),
             pltpu.VMEM((16, 16, 512), jnp.int16),
@@ -542,37 +544,37 @@
         out_specs=[vmem] * 2,
         scratch_shapes=[
             pltpu.VMEM((16, 256, 256), BF16),
-            pltpu.VMEM((8, 512, 128), BF16),
+            pltpu.VMEM((8, 256, 256), BF16),
             pltpu.VMEM((8, 256, 256), BF16),
             pltpu.VMEM((8, 256, 256), BF16),
             pltpu.VMEM((6, 256, 256), BF16),
             pltpu.VMEM((2, 256, 256), BF16),
             pltpu.VMEM((256, 256), F32),
-            pltpu.VMEM((6, 512, 128), BF16),
-            pltpu.VMEM((2, 512, 128), BF16),
-            pltpu.VMEM((512, 128), F32),
+            pltpu.VMEM((6, 256, 256), BF16),
+            pltpu.VMEM((2, 256, 256), BF16),
+            pltpu.VMEM((256, 256), F32),
             pltpu.SemaphoreType.DMA((n,)),
             pltpu.SemaphoreType.DMA((n,)),
         ],
         compiler_params=pltpu.CompilerParams(
             collective_id=collective_id, has_side_effects=True, vmem_limit_bytes=12 * MIB
         ),
-    )(rp.reshape(16, 256, 256), cp.reshape(8, 512, 128))
+    )(rp.reshape(16, 256, 256), cp.reshape(8, 256, 256))
     return u.reshape(32, 128, 256), v.reshape(16, 256, 128)
 
 
 def local(counts, whiten, initial_tiles, tile_rows, tile_cols, tile_count):
     where_at = jnp.stack([lax.axis_index("row") * 32, lax.axis_index("col") * 16]).astype(jnp.int32)
     scalars = (tile_rows.reshape(96), tile_cols.reshape(96), tile_count.reshape(1), where_at)
-    xr, xc, xrt, xct, tiles = prep(counts, whiten, initial_tiles.reshape(96, 128, 128))
-    xr, xc = xr.reshape(32, 256, 128), xc.reshape(16, 256, 128)
+    xc, xrt, xct, tiles = prep(counts, whiten, initial_tiles.reshape(96, 128, 128))
+    xc = xc.reshape(16, 256, 128)
     xrt, xct = xrt.reshape(32, 128, 256), xct.reshape(16, 128, 256)
     omega_shape = jax.ShapeDtypeStruct(tiles.shape, F32)
-    part_shapes = [jax.ShapeDtypeStruct((32, 128, 256), F32), jax.ShapeDtypeStruct((16, 256, 128), F32)]
-    rp, cp = tile_call(first_kernel, scalars, (tiles, xr, xct), part_shapes, pltpu.VMEM, [], 10)
+    part_shapes = [jax.ShapeDtypeStruct((n, 128, 256), F32) for n in (32, 16)]
+    rp, cp = tile_call(first_kernel, scalars, (tiles, xrt, xct), part_shapes, pltpu.VMEM, [], 10)
     u, v = reduce_both(rp, cp, 1)
     omega, rp, cp = tile_call(
-        middle_kernel, scalars, (tiles, u, v, xrt, xc, xr, xct), [omega_shape] + part_shapes, pltpu.VMEM,
+        middle_kernel, scalars, (tiles, u, v, xrt, xc, xct), [omega_shape] + part_shapes, pltpu.VMEM,
         [pltpu.VMEM((GROUP, 128, 128), F32)], 10,
     )
     u, v = reduce_both(rp, cp, 2)

time: 129 us -> 128 us (level)
    pallas_call x3, Pallas kernels: 20.4 us -> 15 us  [tile_call(): pl.pallas_call(kernel, out_shape=out_shape, in_specs=[smem] * 4 + [vmem]...]
    pallas_call x2, Pallas kernels: 70.2 us -> 74.4 us  [reduce_both(): pl.pallas_call(reduce_kernel, out_shape=[jax.ShapeDtypeStruct((16, 256, 2...]
where the time goes in v4:
time: 128 us
  Pallas kernels  124 us (97%)
  local copies, waits for them, and re-layouts  2.03 us (2%)
  between operations  1.59 us (1%)
    pallas_call x2, Pallas kernels, reduce_both(): pl.pallas_call(reduce_kernel, out_shape=[jax.ShapeDtypeStruct((16, 256, 2...  74.4 us
    pallas_call x1, Pallas kernels, prep(): pl.pallas_call(prep_kernel, out_shape=[jax.ShapeDtypeStruct(s, BF16) for...  34.5 us
    pallas_call x3, Pallas kernels, tile_call(): pl.pallas_call(kernel, out_shape=out_shape, in_specs=[smem] * 4 + [vmem]...  15 us

profile of v4, /device:TPU:1, one launch (start us, length us, event | category | flops | bytes accessed | tf_op | source)
XLA Modules:
  0.0 127.6 jit_solution(7646648090630981999)
XLA Ops:
  0.6 0.0 copy-start.2
  0.6 0.0 copy-start.1
  1.4 0.1 pad_add_fusion.where_at
  1.4 1.1 dynamic-slice_bitcast_fusion.whiten
  2.5 0.0 copy-start
  2.5 0.9 copy-done
  3.5 34.5 %shard_map.77 = (bf16[8,512,128]{2,1,0:T(8,128)(2,1)S(1)}, bf16[16,256,256]{2,1,0:T(8,128)(2,1)S(1)}, bf16[8,256,256]{2,1,0:T(8,128)(2,1)S(1)}, f32[96,128,128]{2,1,0:T(8,128)S(1)}) custom-call(s32[16,4096]{1,0:T(8,128)S(1)} %copy-done, f32[96,128,128]{2,1,0:T(8,128)} %bitcast.45, bf16[512,512]{1,0:T(8,128)(2,1)S(1)} %dynamic-slice_bitcast_fusion.whiten), custom_call_target="tpu_custom_call" | custom-call | tf_op jit(solution)/shard_map/pallas_call | solution.py:518
  37.9 0.0 copy-done.2
  38.0 0.0 copy-done.1
  38.0 3.2 %shard_map.78 = (f32[32,128,256]{2,1,0:T(8,128)S(1)}, f32[16,128,256]{2,1,0:T(8,128)S(1)}) custom-call(s32[96]{0:T(128)S(1)} %bitcast.39, s32[96]{0:T(128)S(1)} %bitcast.42, s32[1]{0:T(128)} %bitcast.21.count, s32[2]{0:T(128)S(1)} %pad_add_fusion.where_at, f32[96,128,128]{2,1,0:T(8,128)S(1)} %get-tuple-element.17.tiles, bf16[32,128,256]{2,1,0:T(8,128)(2,1)S(1)} %bitcast.24, ...), custom_call_target="tpu_custom_call" | custom-call | tf_op jit(solution)/shard_map/pallas_call | solution.py:503
  41.1 38.6 %shard_map.79 = (bf16[16,256,256]{2,1,0:T(8,128)(2,1)S(1)}, bf16[8,512,128]{2,1,0:T(8,128)(2,1)S(1)}) custom-call(f32[16,256,256]{2,1,0:T(8,128)S(1)} %bitcast.30, f32[8,256,256]{2,1,0:T(8,128)S(1)} %bitcast.34), custom_call_target="tpu_custom_call" | custom-call | tf_op jit(solution)/shard_map/pallas_call | solution.py:540
  79.7 6.3 %shard_map.80 = (f32[96,128,128]{2,1,0:T(8,128)S(1)}, f32[32,128,256]{2,1,0:T(8,128)S(1)}, f32[16,128,256]{2,1,0:T(8,128)S(1)}) custom-call(s32[96]{0:T(128)S(1)} %bitcast.40, s32[96]{0:T(128)S(1)} %bitcast.43, s32[1]{0:T(128)} %bitcast.22.count, s32[2]{0:T(128)S(1)} %pad_add_fusion.where_at, f32[96,128,128]{2,1,0:T(8,128)S(1)} %get-tuple-element.17.tiles, ...), custom_call_target="tpu_custom_call" | custom-call | tf_op jit(solution)/shard_map/pallas_call | solution.py:503
  86.1 35.8 %shard_map.81 = (bf16[16,256,256]{2,1,0:T(8,128)(2,1)S(1)}, bf16[8,512,128]{2,1,0:T(8,128)(2,1)S(1)}) custom-call(f32[16,256,256]{2,1,0:T(8,128)S(1)} %bitcast.29, f32[8,256,256]{2,1,0:T(8,128)S(1)} %bitcast.33), custom_call_target="tpu_custom_call" | custom-call | tf_op jit(solution)/shard_map/pallas_call | solution.py:540
  121.9 5.6 %shard_map.82 = (f32[96,128,128]{2,1,0:T(8,128)}, f32[96,128,128]{2,1,0:T(8,128)}) custom-call(s32[96]{0:T(128)S(1)} %bitcast.41, s32[96]{0:T(128)S(1)} %bitcast.44, s32[1]{0:T(128)} %bitcast.23.count, s32[2]{0:T(128)S(1)} %pad_add_fusion.where_at, f32[96,128,128]{2,1,0:T(8,128)S(1)} %get-tuple-element.25.tiles, bf16[32,128,256]{2,1,0:T(8,128)(2,1)S(1)} %bitcast.35, ...), custom_call_target="tpu_custom_call" | custom-call | tf_op jit(solution)/shard_map/pallas_call | solution.py:503
Async XLA Ops:
  0.6 37.3 %copy-start.2 = (s32[1,1,96]{2,1,0:T(1,128)S(1)}, s32[1,1,96]{2,1,0:T(1,128)}, u32[]{:S(2)}) copy-start(s32[1,1,96]{2,1,0:T(1,128)} %param.10) | copy-start | bytes 1156
  0.6 37.3 %copy-start.1 = (s32[1,1,96]{2,1,0:T(1,128)S(1)}, s32[1,1,96]{2,1,0:T(1,128)}, u32[]{:S(2)}) copy-start(s32[1,1,96]{2,1,0:T(1,128)} %param.9) | copy-start | bytes 1156
  2.5 1.0 copy-start

commit v5 on v4

--- a/solution.py
+++ b/solution.py
@@ -124,15 +124,6 @@
         for d, other in self.shared:
             self.w.recv(f"{self.tag}core{d}{other}")
             self.done(self.slot(d, other) + 8 - 2 * self.base)
-
-
-def arrivals(gathers):
-    for other in (0, 1):
-        for d in (1, 3, 2):
-            for gather in gathers:
-                gather.arrive(other, d)
-    for gather in gathers:
-        gather.rest()
 
 
 def row_gather(wire, stream, place, out, done, relayed):
@@ -312,7 +303,65 @@
         self.stream.cut(out, slot)[...] = total.T if turned else total
 
 
-def reduce_kernel(rfull, cfull, u, v, rp, cp, pair, summed, rland, rtemp, rkeep, cland, ctemp, ckeep, send_sem, recv_sem):
+class ZFirst:
+    def __init__(self, wire, stream, place, summed, slot, zin, sums, xin, keep, out):
+        self.w, self.stream, self.place, self.tag = wire, stream, place, f"zf{stream.part}"
+        self.summed, self.slot, self.zin, self.sums, self.xin = summed, slot, zin, sums, xin
+        self.keep, self.out, self.shared = keep, out, []
+
+    def cross(self, d):
+        src = self.stream.cut(self.summed, self.slot(d, 1 - self.place.zl))
+        self.w.send(f"{self.tag}z{d}", src, self.stream.cut(self.zin, d), self.place.zlpeer())
+
+    def merge(self, d):
+        self.w.recv(f"{self.tag}z{d}")
+        mine = self.stream.cut(self.summed, self.slot(d, self.place.zl))[...]
+        total = add(mine, self.stream.cut(self.zin, d)[...])
+        if d == 0:
+            self.keep[self.stream.rows(self.keep)] = total
+            return
+        out = self.stream.cut(self.sums, d - 1)
+        out[...] = total.astype(BF16)
+        self.w.send(f"{self.tag}x{d}", out, self.stream.cut(self.xin, d - 1), self.place.xpeer(d))
+
+    def last(self):
+        parts = [self.keep[self.stream.rows(self.keep)]]
+        for d in (1, 2, 3):
+            self.w.recv(f"{self.tag}x{d}")
+            parts.append(self.stream.cut(self.xin, d - 1)[...])
+        self.stream.cut(self.out, self.place.mine)[...] = add(*parts).astype(BF16)
+        for d in (1, 3, 2):
+            self.pass_on(f"g{d}", self.at(0, 0), self.place.xpeer(d))
+        self.pass_on("c0", self.at(0, 0), self.place.zlpeer())
+        self.have(0, 0)
+
+    def at(self, d, other):
+        z = 1 - self.place.zl if other else self.place.zl
+        return self.place.core * 8 + ((self.place.x + d) % 4) * 2 + z
+
+    def pass_on(self, name, slot, device):
+        part = self.stream.cut(self.out, slot)
+        self.w.send(self.tag + name, part, part, device)
+
+    def have(self, d, other):
+        self.pass_on(f"core{d}{other}", self.at(d, other), self.place.sibling())
+        self.shared.append((d, other))
+
+    def near(self, d):
+        self.w.recv(f"{self.tag}g{d}")
+        self.pass_on(f"c{4 - d}", self.at(4 - d, 0), self.place.zlpeer())
+        self.have(4 - d, 0)
+
+    def beyond(self, d):
+        self.w.recv(f"{self.tag}c{d}")
+        self.have(d, 1)
+
+    def rest(self):
+        for d, other in self.shared:
+            self.w.recv(f"{self.tag}core{d}{other}")
+
+
+def reduce_kernel(rfull, cfull, u, v, rp, cp, pair, summed, rland, rtemp, rkeep, zin, sums, xin, cland, ctemp, ckeep, send_sem, recv_sem):
     place = Place()
     peers = [place.sibling(), place.zlpeer(), place.zhpeer()]
     peers += [place.xpeer(d) for d in (1, 2, 3)] + [place.ypeer(d) for d in (1, 2, 3)]
@@ -333,10 +382,8 @@
     cols = [
         Scatter(wire, t, "cs", cp, cslot, cland, ctemp, ckeep, place.zh, place.ypeer, place.zhpeer()) for t in streams
     ]
-    rows = [
-        Scatter(wire, t, "rs", summed, rslot, rland, rtemp, rkeep, place.zl, place.xpeer, place.zlpeer())
-        for t in streams
-    ]
+    row = Scatter(wire, streams[0], "rs", summed, rslot, rland, rtemp, rkeep, place.zl, place.xpeer, place.zlpeer())
+    other = ZFirst(wire, streams[1], place, summed, rslot, zin, sums, xin, rkeep, u)
     order = ((2, 0), (2, 1), (1, 1), (3, 0), (1, 0), (3, 1), (0, 0), (0, 1))
     for t in streams:
         for d, e in order:
@@ -352,36 +399,61 @@
             wire.recv(f"s{t.part}{d}{e}")
             t.cut(summed, s)[...] = add(t.cut(rp, here + s)[...], t.cut(pair, s)[...]).astype(BF16)
 
-    for t, row in zip(streams, rows):
-        join(t, order[:2])
-        row.first()
-        join(t, order[2:4])
-        row.second()
-    for t, row, col in zip(streams, rows, cols):
-        col.merge()
-        join(t, order[4:6])
-        row.merge()
-    for t in streams:
-        join(t, order[6:])
-    for row, col in zip(rows, cols):
-        col.cross()
-        row.cross()
+    one, two = streams
+    join(one, order[:2])
+    row.first()
+    join(two, order[:2])
+    other.cross(2)
+    join(one, order[2:4])
+    row.second()
+    join(two, order[2:6])
+    other.cross(1)
+    other.cross(3)
+    join(two, order[6:])
+    other.cross(0)
+    cols[0].merge()
+    join(one, order[4:6])
+    row.merge()
+    other.merge(2)
+    cols[1].merge()
+    other.merge(1)
+    other.merge(3)
+    join(one, order[6:])
+    cols[0].cross()
+    row.cross()
+    other.merge(0)
+    cols[1].cross()
     nothing = lambda s: None
-    rgs = [row_gather(wire, t, place, u, nothing, False) for t in streams]
+    rg = row_gather(wire, one, place, u, nothing, False)
     cgs = [col_gather(wire, t, place, v, nothing, False) for t in streams]
-    for row, col, rg, cg in zip(rows, cols, rgs, cgs):
-        col.last(v, place.mine_col, True)
-        cg.exchange(place.zhpeer())
-        cg.start(0)
-        row.last(u, place.mine, False)
-        rg.exchange(place.zlpeer())
-        rg.start(0)
-    for rg, cg in zip(rgs, cgs):
-        cg.exchanged()
-        cg.start(1)
-        rg.exchanged()
-        rg.start(1)
-    arrivals(cgs + rgs)
+    for i in range(2):
+        cols[i].last(v, place.mine_col, True)
+        cgs[i].exchange(place.zhpeer())
+        cgs[i].start(0)
+        if i == 0:
+            row.last(u, place.mine, False)
+            rg.exchange(place.zlpeer())
+            rg.start(0)
+        else:
+            other.last()
+    for d in (1, 3, 2):
+        cgs[0].arrive(0, d)
+        rg.arrive(0, d)
+    for g in (cgs[0], rg, cgs[1]):
+        g.exchanged()
+        g.start(1)
+    for d in (1, 3, 2):
+        other.near(d)
+        cgs[1].arrive(0, d)
+    other.beyond(0)
+    for d in (1, 3, 2):
+        cgs[0].arrive(1, d)
+        rg.arrive(1, d)
+    for d in (3, 1, 2):
+        other.beyond(d)
+        cgs[1].arrive(1, d)
+    rg.rest()
+    other.rest()
     wire.drain()
 
 
@@ -550,6 +622,9 @@
             pltpu.VMEM((6, 256, 256), BF16),
             pltpu.VMEM((2, 256, 256), BF16),
             pltpu.VMEM((256, 256), F32),
+            pltpu.VMEM((4, 256, 256), BF16),
+            pltpu.VMEM((3, 256, 256), BF16),
+            pltpu.VMEM((3, 256, 256), BF16),
             pltpu.VMEM((6, 256, 256), BF16),
             pltpu.VMEM((2, 256, 256), BF16),
             pltpu.VMEM((256, 256), F32),

time: 128 us -> 127 us (level)
    pallas_call x2, Pallas kernels: 74.4 us -> 69.1 us  [reduce_both(): pl.pallas_call(reduce_kernel, out_shape=[jax.ShapeDtypeStruct((16, 256, 2...]
    pallas_call x3, Pallas kernels: 15 us -> 19.7 us  [tile_call(): pl.pallas_call(kernel, out_shape=out_shape, in_specs=[smem] * 4 + [vmem]...]
where the time goes in v5:
time: 127 us
  Pallas kernels  123 us (97%)
  local copies, waits for them, and re-layouts  2.03 us (2%)
  between operations  1.59 us (1%)
    pallas_call x2, Pallas kernels, reduce_both(): pl.pallas_call(reduce_kernel, out_shape=[jax.ShapeDtypeStruct((16, 256, 2...  69.1 us
    pallas_call x1, Pallas kernels, prep(): pl.pallas_call(prep_kernel, out_shape=[jax.ShapeDtypeStruct(s, BF16) for...  34.5 us
    pallas_call x3, Pallas kernels, tile_call(): pl.pallas_call(kernel, out_shape=out_shape, in_specs=[smem] * 4 + [vmem]...  19.7 us

profile of v5, /device:TPU:1, one launch (start us, length us, event | category | flops | bytes accessed | tf_op | source)
XLA Modules:
  0.0 127.0 jit_solution(12249573070171549314)
XLA Ops:
  0.6 0.0 copy-start.2
  0.6 0.0 copy-start.1
  1.4 0.1 pad_add_fusion.where_at
  1.4 1.1 dynamic-slice_bitcast_fusion.whiten
  2.5 0.0 copy-start
  2.5 0.9 copy-done
  3.5 34.5 %shard_map.77 = (bf16[8,512,128]{2,1,0:T(8,128)(2,1)S(1)}, bf16[16,256,256]{2,1,0:T(8,128)(2,1)S(1)}, bf16[8,256,256]{2,1,0:T(8,128)(2,1)S(1)}, f32[96,128,128]{2,1,0:T(8,128)S(1)}) custom-call(s32[16,4096]{1,0:T(8,128)S(1)} %copy-done, f32[96,128,128]{2,1,0:T(8,128)} %bitcast.45, bf16[512,512]{1,0:T(8,128)(2,1)S(1)} %dynamic-slice_bitcast_fusion.whiten), custom_call_target="tpu_custom_call" | custom-call | tf_op jit(solution)/shard_map/pallas_call | solution.py:590
  37.9 0.0 copy-done.2
  38.0 0.0 copy-done.1
  38.0 4.3 %shard_map.78 = (f32[32,128,256]{2,1,0:T(8,128)S(1)}, f32[16,128,256]{2,1,0:T(8,128)S(1)}) custom-call(s32[96]{0:T(128)S(1)} %bitcast.39, s32[96]{0:T(128)S(1)} %bitcast.42, s32[1]{0:T(128)} %bitcast.21.count, s32[2]{0:T(128)S(1)} %pad_add_fusion.where_at, f32[96,128,128]{2,1,0:T(8,128)S(1)} %get-tuple-element.17.tiles, bf16[32,128,256]{2,1,0:T(8,128)(2,1)S(1)} %bitcast.24, ...), custom_call_target="tpu_custom_call" | custom-call | tf_op jit(solution)/shard_map/pallas_call | solution.py:575
  42.2 35.6 %shard_map.79 = (bf16[16,256,256]{2,1,0:T(8,128)(2,1)S(1)}, bf16[8,512,128]{2,1,0:T(8,128)(2,1)S(1)}) custom-call(f32[16,256,256]{2,1,0:T(8,128)S(1)} %bitcast.30, f32[8,256,256]{2,1,0:T(8,128)S(1)} %bitcast.34), custom_call_target="tpu_custom_call" | custom-call | tf_op jit(solution)/shard_map/pallas_call | solution.py:612
  77.8 8.6 %shard_map.80 = (f32[96,128,128]{2,1,0:T(8,128)S(1)}, f32[32,128,256]{2,1,0:T(8,128)S(1)}, f32[16,128,256]{2,1,0:T(8,128)S(1)}) custom-call(s32[96]{0:T(128)S(1)} %bitcast.40, s32[96]{0:T(128)S(1)} %bitcast.43, s32[1]{0:T(128)} %bitcast.22.count, s32[2]{0:T(128)S(1)} %pad_add_fusion.where_at, f32[96,128,128]{2,1,0:T(8,128)S(1)} %get-tuple-element.17.tiles, ...), custom_call_target="tpu_custom_call" | custom-call | tf_op jit(solution)/shard_map/pallas_call | solution.py:575
  86.5 33.5 %shard_map.81 = (bf16[16,256,256]{2,1,0:T(8,128)(2,1)S(1)}, bf16[8,512,128]{2,1,0:T(8,128)(2,1)S(1)}) custom-call(f32[16,256,256]{2,1,0:T(8,128)S(1)} %bitcast.29, f32[8,256,256]{2,1,0:T(8,128)S(1)} %bitcast.33), custom_call_target="tpu_custom_call" | custom-call | tf_op jit(solution)/shard_map/pallas_call | solution.py:612
  120.0 6.9 %shard_map.82 = (f32[96,128,128]{2,1,0:T(8,128)}, f32[96,128,128]{2,1,0:T(8,128)}) custom-call(s32[96]{0:T(128)S(1)} %bitcast.41, s32[96]{0:T(128)S(1)} %bitcast.44, s32[1]{0:T(128)} %bitcast.23.count, s32[2]{0:T(128)S(1)} %pad_add_fusion.where_at, f32[96,128,128]{2,1,0:T(8,128)S(1)} %get-tuple-element.25.tiles, bf16[32,128,256]{2,1,0:T(8,128)(2,1)S(1)} %bitcast.35, ...), custom_call_target="tpu_custom_call" | custom-call | tf_op jit(solution)/shard_map/pallas_call | solution.py:575
Async XLA Ops:
  0.6 37.3 %copy-start.2 = (s32[1,1,96]{2,1,0:T(1,128)S(1)}, s32[1,1,96]{2,1,0:T(1,128)}, u32[]{:S(2)}) copy-start(s32[1,1,96]{2,1,0:T(1,128)} %param.10) | copy-start | bytes 1156
  0.6 37.3 %copy-start.1 = (s32[1,1,96]{2,1,0:T(1,128)S(1)}, s32[1,1,96]{2,1,0:T(1,128)}, u32[]{:S(2)}) copy-start(s32[1,1,96]{2,1,0:T(1,128)} %param.9) | copy-start | bytes 1156
  2.5 1.0 copy-start

commit v6 on v5

--- a/solution.py
+++ b/solution.py
@@ -436,12 +436,14 @@
             rg.start(0)
         else:
             other.last()
+    for g in (cgs[0], rg):
+        g.exchanged()
+        g.start(1)
     for d in (1, 3, 2):
         cgs[0].arrive(0, d)
         rg.arrive(0, d)
-    for g in (cgs[0], rg, cgs[1]):
-        g.exchanged()
-        g.start(1)
+    cgs[1].exchanged()
+    cgs[1].start(1)
     for d in (1, 3, 2):
         other.near(d)
         cgs[1].arrive(0, d)

time: 127 us -> 126 us (level)
    pallas_call x3, Pallas kernels: 19.7 us -> 15 us  [tile_call(): pl.pallas_call(kernel, out_shape=out_shape, in_specs=[smem] * 4 + [vmem]...]
    pallas_call x2, Pallas kernels: 69.1 us -> 72.2 us  [reduce_both(): pl.pallas_call(reduce_kernel, out_shape=[jax.ShapeDtypeStruct((16, 256, 2...]
where the time goes in v6:
time: 126 us; the launch traced here: 125 us
  Pallas kernels  122 us (97%)
  local copies, waits for them, and re-layouts  2.03 us (2%)
  between operations  1.59 us (1%)
    pallas_call x2, Pallas kernels, reduce_both(): pl.pallas_call(reduce_kernel, out_shape=[jax.ShapeDtypeStruct((16, 256, 2...  72.2 us
    pallas_call x1, Pallas kernels, prep(): pl.pallas_call(prep_kernel, out_shape=[jax.ShapeDtypeStruct(s, BF16) for...  34.5 us
    pallas_call x3, Pallas kernels, tile_call(): pl.pallas_call(kernel, out_shape=out_shape, in_specs=[smem] * 4 + [vmem]...  15 us

profile of v6, /device:TPU:1, one launch (start us, length us, event | category | flops | bytes accessed | tf_op | source)
XLA Modules:
  0.0 125.4 jit_solution(14452416578889097275)
XLA Ops:
  0.6 0.0 copy-start.2
  0.6 0.0 copy-start.1
  1.4 0.1 pad_add_fusion.where_at
  1.4 1.1 dynamic-slice_bitcast_fusion.whiten
  2.5 0.0 copy-start
  2.5 0.9 copy-done
  3.5 34.5 %shard_map.77 = (bf16[8,512,128]{2,1,0:T(8,128)(2,1)S(1)}, bf16[16,256,256]{2,1,0:T(8,128)(2,1)S(1)}, bf16[8,256,256]{2,1,0:T(8,128)(2,1)S(1)}, f32[96,128,128]{2,1,0:T(8,128)S(1)}) custom-call(s32[16,4096]{1,0:T(8,128)S(1)} %copy-done, f32[96,128,128]{2,1,0:T(8,128)} %bitcast.45, bf16[512,512]{1,0:T(8,128)(2,1)S(1)} %dynamic-slice_bitcast_fusion.whiten), custom_call_target="tpu_custom_call" | custom-call | tf_op jit(solution)/shard_map/pallas_call | solution.py:592
  37.9 0.0 copy-done.2
  38.0 0.0 copy-done.1
  38.0 3.2 %shard_map.78 = (f32[32,128,256]{2,1,0:T(8,128)S(1)}, f32[16,128,256]{2,1,0:T(8,128)S(1)}) custom-call(s32[96]{0:T(128)S(1)} %bitcast.39, s32[96]{0:T(128)S(1)} %bitcast.42, s32[1]{0:T(128)} %bitcast.21.count, s32[2]{0:T(128)S(1)} %pad_add_fusion.where_at, f32[96,128,128]{2,1,0:T(8,128)S(1)} %get-tuple-element.17.tiles, bf16[32,128,256]{2,1,0:T(8,128)(2,1)S(1)} %bitcast.24, ...), custom_call_target="tpu_custom_call" | custom-call | tf_op jit(solution)/shard_map/pallas_call | solution.py:577
  41.1 38.1 %shard_map.79 = (bf16[16,256,256]{2,1,0:T(8,128)(2,1)S(1)}, bf16[8,512,128]{2,1,0:T(8,128)(2,1)S(1)}) custom-call(f32[16,256,256]{2,1,0:T(8,128)S(1)} %bitcast.30, f32[8,256,256]{2,1,0:T(8,128)S(1)} %bitcast.34), custom_call_target="tpu_custom_call" | custom-call | tf_op jit(solution)/shard_map/pallas_call | solution.py:614
  79.2 6.3 %shard_map.80 = (f32[96,128,128]{2,1,0:T(8,128)S(1)}, f32[32,128,256]{2,1,0:T(8,128)S(1)}, f32[16,128,256]{2,1,0:T(8,128)S(1)}) custom-call(s32[96]{0:T(128)S(1)} %bitcast.40, s32[96]{0:T(128)S(1)} %bitcast.43, s32[1]{0:T(128)} %bitcast.22.count, s32[2]{0:T(128)S(1)} %pad_add_fusion.where_at, f32[96,128,128]{2,1,0:T(8,128)S(1)} %get-tuple-element.17.tiles, ...), custom_call_target="tpu_custom_call" | custom-call | tf_op jit(solution)/shard_map/pallas_call | solution.py:577
  85.5 34.2 %shard_map.81 = (bf16[16,256,256]{2,1,0:T(8,128)(2,1)S(1)}, bf16[8,512,128]{2,1,0:T(8,128)(2,1)S(1)}) custom-call(f32[16,256,256]{2,1,0:T(8,128)S(1)} %bitcast.29, f32[8,256,256]{2,1,0:T(8,128)S(1)} %bitcast.33), custom_call_target="tpu_custom_call" | custom-call | tf_op jit(solution)/shard_map/pallas_call | solution.py:614
  119.7 5.6 %shard_map.82 = (f32[96,128,128]{2,1,0:T(8,128)}, f32[96,128,128]{2,1,0:T(8,128)}) custom-call(s32[96]{0:T(128)S(1)} %bitcast.41, s32[96]{0:T(128)S(1)} %bitcast.44, s32[1]{0:T(128)} %bitcast.23.count, s32[2]{0:T(128)S(1)} %pad_add_fusion.where_at, f32[96,128,128]{2,1,0:T(8,128)S(1)} %get-tuple-element.25.tiles, bf16[32,128,256]{2,1,0:T(8,128)(2,1)S(1)} %bitcast.35, ...), custom_call_target="tpu_custom_call" | custom-call | tf_op jit(solution)/shard_map/pallas_call | solution.py:577
Async XLA Ops:
  0.6 37.3 %copy-start.2 = (s32[1,1,96]{2,1,0:T(1,128)S(1)}, s32[1,1,96]{2,1,0:T(1,128)}, u32[]{:S(2)}) copy-start(s32[1,1,96]{2,1,0:T(1,128)} %param.10) | copy-start | bytes 1156
  0.6 37.3 %copy-start.1 = (s32[1,1,96]{2,1,0:T(1,128)S(1)}, s32[1,1,96]{2,1,0:T(1,128)}, u32[]{:S(2)}) copy-start(s32[1,1,96]{2,1,0:T(1,128)} %param.9) | copy-start | bytes 1156
  2.5 1.0 copy-start
